TPU v7x, 32 devices: a whole 2x2x4 slice. The times are simulated.
32 devices in a mesh: group: 2 (over x), gz: 16 (over z, y, core).
Axes of the slice: x: 2, y: 2, z: 4, core: 2. Of those that a mesh axis runs over, the one named last changes fastest.
Arguments:
- velocity: float32 [2, 3, 32, 256, 256], P('group', None, 'gz'), may hold values from -5 to 5
- fringe_start: int32 [1], replicated, may hold values from 0 to 224
- turbine_level: int32 [64], replicated, may hold values from 0 to 31
- turbine_row: int32 [64], replicated, may hold values from 0 to 255
- turbine_col: int32 [64], replicated, may hold values from 0 to 255
- thrust: float32 [64], replicated, may hold values from 1 to 12
- green_basis: float32 [32, 32], replicated, may hold values from -0.5 to 2.5
- eigen_shift: float32 [32], replicated, may hold values from 0.05 to 1
Outputs:
- updated: float32 [2, 3, 32, 256, 256], P('group', None, 'gz')
- pressure: float32 [2, 32, 256, 256], P('group', 'gz')
All inputs are finite; a program needn't handle non-finite values.
Results may differ from a plain program's by a relative error of at most 0.00011.
Values sent between devices are 32-bit elements; how exact they have to be, the bound alone decides.
A program may use at most 64 MiB of HBM per device.

v0:
```python
import jax
import jax.numpy as jnp
from jax import lax
from jax.sharding import PartitionSpec as P

FRINGE = 32


highest = lax.Precision.HIGHEST
time_step = 0.25


def padded(cells, sides, width):
    for axis, dim in sides:
        count = lax.axis_size(axis)
        ends = count - 1
        head = lax.slice_in_dim(cells, 0, width, axis=dim)
        tail = lax.slice_in_dim(cells, cells.shape[dim] - width, cells.shape[dim], axis=dim)
        cells = jnp.concatenate(
            [
                lax.ppermute(tail, axis, [(i, (i + 1) % count) for i in range(ends)]),
                cells,
                lax.ppermute(head, axis, [((i + 1) % count, i) for i in range(ends)]),
            ],
            axis=dim,
        )
    return cells


def from_behind(value, axis, by):
    size = lax.axis_size(axis)
    pairs = [(i, i + by) for i in range(size) if 0 <= i + by < size]
    return lax.ppermute(value, axis, pairs)


def wavenumber(ids, length):
    middle = length // 2
    return jnp.where(ids <= middle, ids, ids - middle)


def real_basis(length):
    row_ids = jnp.arange(length, dtype=jnp.int32)[:, None]
    col_ids = jnp.arange(length, dtype=jnp.int32)[None, :]
    middle = length // 2
    phases = (
        2.0 * jnp.pi / length * (wavenumber(row_ids, length) * col_ids % length).astype(jnp.float32)
    )
    edges = (row_ids == 0) | (row_ids == middle)
    weights_norm = jnp.sqrt(jnp.where(edges, 1.0, 2.0) / length)
    return jnp.where(row_ids <= middle, jnp.cos(phases), jnp.sin(phases)) * weights_norm


def derivative(length):
    row_ids = jnp.arange(length, dtype=jnp.int32)[:, None]
    col_ids = jnp.arange(length, dtype=jnp.int32)[None, :]
    middle = length // 2
    omega_upper = 2.0 * jnp.pi / length * row_ids.astype(jnp.float32)
    omega_lower = 2.0 * jnp.pi / length * (row_ids - middle).astype(jnp.float32)
    upper = jnp.where(
        (row_ids >= 1) & (row_ids < middle) & (col_ids == row_ids + middle), omega_upper, 0.0
    )
    lower = jnp.where((row_ids > middle) & (col_ids == row_ids - middle), -omega_lower, 0.0)
    basis = real_basis(length)
    return jnp.dot(basis.T, jnp.dot(upper + lower, basis, precision=highest), precision=highest)


def wave_square(ids, length):
    wave = wavenumber(ids, length).astype(jnp.float32) * (2.0 * jnp.pi / length)
    return wave * wave


def x_derivative(field, matrix):
    return jnp.einsum("...yb,ab->...ya", field, matrix, precision=highest)


def y_derivative(field, matrix):
    return jnp.einsum("ab,...bx->...ax", matrix, field, precision=highest)


def forward_plane(field, basis_y, basis_x):
    return x_derivative(y_derivative(field, basis_y), basis_x)


def inverse_plane(field, basis_y, basis_x):
    return x_derivative(y_derivative(field, basis_y.T), basis_x.T)


def advection(fields, vertical, deriv_y, deriv_x):
    along_x = x_derivative(fields, deriv_x)
    along_y = y_derivative(fields, deriv_y)
    return -(fields[0:1] * along_x + fields[1:2] * along_y + fields[2:3] * vertical)


def fringe_shape(offset):
    sine_part = jnp.sin(jnp.pi * (offset + 0.5) / FRINGE)
    return sine_part * sine_part


def turbine_force(speed, level_local, turbine_row, turbine_col, thrust):
    levels_here, rows_y, cols_x = speed.shape
    pick_level = (level_local[:, None] == jnp.arange(levels_here, dtype=jnp.int32)[None, :]).astype(
        jnp.float32
    )
    pick_row = (turbine_row[:, None] == jnp.arange(rows_y, dtype=jnp.int32)[None, :]).astype(
        jnp.float32
    )
    pick_col = (turbine_col[:, None] == jnp.arange(cols_x, dtype=jnp.int32)[None, :]).astype(
        jnp.float32
    )
    row_pick = jnp.einsum("ty,lyx->tlx", pick_row, speed, precision=highest)
    cell_speed = jnp.sum(row_pick * pick_level[:, :, None] * pick_col[:, None, :], axis=(1, 2))
    drag_force = -thrust * jnp.abs(cell_speed) * cell_speed
    placed = pick_level[:, :, None] * (drag_force[:, None, None] * pick_row[:, None, :])
    return jnp.einsum("tly,tx->lyx", placed, pick_col, precision=highest)


def local(
    velocity,
    fringe_start,
    turbine_level,
    turbine_row,
    turbine_col,
    thrust,
    green_basis,
    eigen_shift,
):
    fields = velocity[0]
    levels_here = fields.shape[1]
    rows_y = fields.shape[2]
    cols_x = fields.shape[3]
    basis_y = real_basis(rows_y)
    basis_x = real_basis(cols_x)
    deriv_y = derivative(rows_y)
    deriv_x = derivative(cols_x)
    is_farm = (lax.axis_index("group") > 0).astype(jnp.float32)
    slab_id = lax.axis_index("gz")
    extended = padded(fields, (("gz", 1),), 2)
    centre_levels = extended[:, 1 : levels_here + 2]
    vertical = 0.5 * (extended[:, 2 : levels_here + 3] - extended[:, 0 : levels_here + 1])
    tendency = advection(centre_levels, vertical, deriv_y, deriv_x)
    level_local = turbine_level - slab_id * levels_here
    force = turbine_force(fields[0], level_local, turbine_row, turbine_col, thrust)
    local_tend = tendency[:, 1:]
    local_tend = jnp.concatenate([local_tend[0:1] + is_farm * force[None], local_tend[1:]], 0)
    predicted = fields + time_step * local_tend
    ghost_upward = extended[2, 1] + time_step * tendency[2, 0]
    fringe_at = fringe_start[0]
    upstream = from_behind(fields[:2], "group", 1)
    offset = jnp.arange(cols_x, dtype=jnp.int32) - fringe_at
    inside = (offset >= 0) & (offset < FRINGE)
    fringe_ramp = jnp.where(inside, fringe_shape(offset.astype(jnp.float32)), 0.0)
    horizontal = predicted[:2] + is_farm * fringe_ramp * (upstream - predicted[:2])
    upward = predicted[2]
    below = jnp.concatenate([ghost_upward[None], upward[:-1]], 0)
    divergence = (
        x_derivative(horizontal[0], deriv_x)
        + y_derivative(horizontal[1], deriv_y)
        + (upward - below)
    )
    spectrum = forward_plane(divergence, basis_y, basis_x).reshape(levels_here, rows_y * cols_x)
    modes = lax.all_to_all(spectrum, "gz", split_axis=1, concat_axis=0, tiled=True)
    per_slab = modes.shape[1]
    mode_ids = slab_id * per_slab + jnp.arange(per_slab, dtype=jnp.int32)
    modes_ksq = wave_square(mode_ids // cols_x, rows_y) + wave_square(mode_ids % cols_x, cols_x)
    scaled = jnp.dot(green_basis, modes, precision=highest) / (
        eigen_shift[:, None] + modes_ksq[None, :]
    )
    pressure_modes = jnp.dot(green_basis.T, scaled, precision=highest)
    planes_p = lax.all_to_all(pressure_modes, "gz", split_axis=0, concat_axis=1, tiled=True)
    pressure = inverse_plane(planes_p.reshape(levels_here, rows_y, cols_x), basis_y, basis_x)
    above = from_behind(pressure[0:1], "gz", -1)
    rise = jnp.concatenate([pressure[1:], above], 0) - pressure
    correction = jnp.stack(
        [x_derivative(pressure, deriv_x), y_derivative(pressure, deriv_y), rise], 0
    )
    updated = jnp.concatenate([horizontal, upward[None]], 0) - correction
    return (updated[None], pressure[None])


def solution(mesh):
    return jax.shard_map(
        local,
        mesh=mesh,
        in_specs=(P("group", None, "gz", None, None), P(), P(), P(), P(), P(), P(), P()),
        out_specs=(P("group", None, "gz", None, None), P("group", "gz", None, None)),
        check_vma=False,
    )
```

profile of v0, /device:TPU:1, one launch (start us, length us, event | category | flops | bytes accessed | tf_op | source)
XLA Modules:
  0.0 111.9 jit_solution(13099789606566363385)
XLA Ops:
  0.6 0.0 copy-start
  0.7 4.7 %collective-permute-start = (f32[3,2,256,256]{3,2,1,0:T(8,128)}, f32[3,2,256,256]{3,2,1,0:T(8,128)S(1)}, u32[]{:S(2)}, u32[]{:S(2)}) collective-permute-start(f32[3,2,256,256]{3,2,1,0:T(8,128)} %bitcast.111), channel_id=1, source_target_pairs={{0,1},{1,2},{2,3},{3,4},{4,5},{5,6},{6,7},{7,8},{8,9},{9,10},{10,1... | collective-permute-start | bytes 4718600 | tf_op jit(solution)/shard_map/ppermute | solution.py:21
  5.4 1.9 %collective-permute-start.1 = (f32[3,2,256,256]{3,2,1,0:T(8,128)}, f32[3,2,256,256]{3,2,1,0:T(8,128)}, u32[]{:S(2)}, u32[]{:S(2)}) collective-permute-start(f32[3,2,256,256]{3,2,1,0:T(8,128)} %bitcast.112), channel_id=1, source_target_pairs={{1,0},{2,1},{3,2},{4,3},{5,4},{6,5},{7,6},{8,7},{9,8},{10,9},{11,1... | collective-permute-start | bytes 4718600 | tf_op jit(solution)/shard_map/ppermute | solution.py:23
  7.3 2.3 %slice_bitcast_fusion = f32[2,2,256,256]{3,2,1,0:T(8,128)} fusion(f32[1,3,2,256,256]{4,3,2,1,0:T(8,128)} %param.8), kind=kLoop, calls=%fused_computation.38 | loop fusion | bytes 2097152 | tf_op jit(solution)/shard_map/slice | solution.py:148
  9.6 4.1 %collective-permute-start.2 = (f32[2,2,256,256]{3,2,1,0:T(8,128)}, f32[2,2,256,256]{3,2,1,0:T(8,128)}, u32[]{:S(2)}, u32[]{:S(2)}) collective-permute-start(f32[2,2,256,256]{3,2,1,0:T(8,128)} %slice_bitcast_fusion), channel_id=1, source_target_pairs={{0,16},{1,17},{2,18},{3,19},{4,20},{5,21},{6,22},{7,23},{8,24},{9,... | collective-permute-start | bytes 3145736 | tf_op jit(solution)/shard_map/ppermute | solution.py:33
  14.4 0.1 fusion.89
  14.5 0.1 fusion.67
  14.6 0.4 fusion.14
  15.1 0.1 fusion.68
  15.1 1.6 %fusion.45 = f32[256,256]{1,0:T(8,128)S(1)} fusion(f32[256]{0:T(256)S(1)} %get-tuple-element.11, s32[256]{0:T(256)S(1)} %get-tuple-element.9, f32[256]{0:T(256)S(1)} %get-tuple-element.12, s32[256]{0:T(256)S(1)} %get-tuple-element.10, pred[256]{0:T(512)(128)(4,1)S(1)} %get-tuple-element.8, pred[256]{0:T(512)(128)(4,1)S(1)} %get-tuple-element.7, ...), kind=kOutput, calls=%fused_computation.80 | convolution fusion | flops 202833920 | bytes 269056 | tf_op jit(solution)/shard_map/dot_general | solution.py:64
  16.8 1.7 %fusion.64 = f32[256,256]{1,0:T(8,128)S(1)} fusion(f32[256,256]{1,0:T(8,128)S(1)} %fusion.45, f32[256]{0:T(256)S(1)} %fusion.88, s32[256]{0:T(256)S(1)} %iota_select_fusion, pred[256]{0:T(512)(128)(4,1)S(1)} %iota_compare_fusion.5), kind=kOutput, calls=%fused_computation.98 | convolution fusion | flops 202375168 | bytes 526592 | tf_op jit(solution)/shard_map/dot_general | solution.py:64
  18.5 21.4 %collective-permute-done = f32[3,2,256,256]{3,2,1,0:T(8,128)S(1)} collective-permute-done((f32[3,2,256,256]{3,2,1,0:T(8,128)}, f32[3,2,256,256]{3,2,1,0:T(8,128)S(1)}, u32[]{:S(2)}, u32[]{:S(2)}) %collective-permute-start) | collective-permute-done | bytes 1572896 | tf_op jit(solution)/shard_map/ppermute | solution.py:21
  39.9 0.2 fusion.16
  40.1 2.2 %fusion.2 = f32[3,3,256,256]{3,2,1,0:T(8,128)S(1)} fusion(f32[3,2,256,256]{3,2,1,0:T(8,128)S(1)} %bitcast.114, f32[3,2,256,256]{3,2,1,0:T(8,128)S(1)} %collective-permute-done, f32[256,256]{1,0:T(8,128)S(1)} %fusion.64), kind=kOutput, calls=%fused_computation.13 | convolution fusion | flops 1812725760 | bytes 5767168 | tf_op jit(solution)/shard_map/...yb,ab->...ya/dot_general | solution.py:73
  42.3 4.9 %fusion.7 = f32[3,3,256,256]{3,2,1,0:T(8,128)S(1)} fusion(f32[3,2,256,256]{3,2,1,0:T(8,128)S(1)} %collective-permute-done, f32[3,2,256,256]{3,2,1,0:T(8,128)S(1)} %bitcast.115, f32[3,2,256,256]{3,2,1,0:T(8,128)} %collective-permute-done.1, f32[3,3,256,256]{3,2,1,0:T(8,128)S(1)} %fusion.2, f32[3,256,256]{2,1,0:T(8,128)S(1)} %get-tuple-element.4, ...), kind=kOutput, calls=%fused_computation.18 | convolution fusion | flops 1818034176 | bytes 15204352 | tf_op jit(solution)/shard_map/ab,...bx->...ax/dot_general | solution.py:77
  47.2 0.1 slice.105
  47.3 0.5 slice_add_fusion
  47.8 0.3 fusion.9
  48.1 0.0 copy-start.2
  48.2 2.0 %multiply_add_fusion = f32[2,2,256,256]{3,2,1,0:T(8,128)S(1)} fusion(f32[2,2,256,256]{3,2,1,0:T(8,128)} %collective-permute-done.2, f32[3,2,256,256]{3,2,1,0:T(8,128)S(1)} %fusion.9, f32[256]{0:T(256)S(1)} %fusion.89), kind=kLoop, calls=%fused_computation.37 | loop fusion | flops 786432 | bytes 3146752 | tf_op jit(solution)/shard_map/add | solution.py:152
  50.1 0.6 fusion.22
  50.7 0.1 fusion.30
  50.8 0.7 fusion.12
  51.5 2.0 %convolution_bitcast_fusion.5 = f32[2,256,256]{1,2,0:T(8,128)S(1)} fusion(f32[2,256,256]{2,1,0:T(8,128)S(1)} %fusion.12, f32[256]{0:T(256)S(1)} %fusion.88, s32[256]{0:T(256)S(1)} %iota_select_fusion, pred[256]{0:T(512)(128)(4,1)S(1)} %iota_compare_fusion.5), kind=kOutput, calls=%fused_computation.28 | convolution fusion | flops 403701760 | bytes 1050880 | tf_op jit(solution)/shard_map/ab,...bx->...ax/dot_general | solution.py:77
  53.5 2.0 %fusion.34 = f32[2,256,256]{2,1,0:T(8,128)S(1)} fusion(f32[2,256,256]{1,2,0:T(8,128)S(1)} %convolution_bitcast_fusion.5, f32[256]{0:T(256)S(1)} %fusion.88, s32[256]{0:T(256)S(1)} %iota_select_fusion, pred[256]{0:T(512)(128)(4,1)S(1)} %iota_compare_fusion.5), kind=kOutput, calls=%fused_computation.71 | convolution fusion | flops 403701760 | bytes 1050880 | tf_op jit(solution)/shard_map/...yb,ab->...ya/dot_general | solution.py:73
  55.6 0.1 all_to_all.26
  55.7 0.0 copy-start.8
  55.7 1.2 %copy.26 = f32[2,16,4096]{2,0,1:T(2,128)} copy(f32[2,16,4096]{2,1,0:T(8,128)S(1)} %all_to_all.26) | data formatting | bytes 1048576 | tf_op jit(solution)/shard_map/all_to_all | solution.py:161
  56.9 6.1 %all-to-all-start = ((f32[2,16,4096]{2,0,1:T(2,128)}), f32[2,16,4096]{2,0,1:T(2,128)S(1)}, u32[]{:S(2)}, u32[]{:S(2)}) async-start(f32[2,16,4096]{2,0,1:T(2,128)} %copy.26), calls=%async_computation | async-start | bytes 1048576 | tf_op jit(solution)/shard_map/all_to_all | solution.py:161
  63.0 14.0 %all-to-all-done = f32[2,16,4096]{2,0,1:T(2,128)S(1)} async-done(((f32[2,16,4096]{2,0,1:T(2,128)}), f32[2,16,4096]{2,0,1:T(2,128)S(1)}, u32[]{:S(2)}, u32[]{:S(2)}) %all-to-all-start) | async-done | bytes 524320 | tf_op jit(solution)/shard_map/all_to_all | solution.py:161
  77.0 0.4 all_to_all.29
  77.4 0.6 fusion
  78.0 0.6 convolution_bitcast_fusion
  78.6 1.1 all_to_all.30
  79.7 4.5 %all-to-all-start.1 = ((f32[16,2,4096]{2,1,0:T(2,128)}), f32[16,2,4096]{2,1,0:T(2,128)S(1)}, u32[]{:S(2)}, u32[]{:S(2)}) async-start(f32[16,2,4096]{2,1,0:T(2,128)} %all_to_all.30), calls=%async_computation.1 | async-start | bytes 1048576 | tf_op jit(solution)/shard_map/all_to_all | solution.py:169
  84.2 1.1 slice_bitcast_fusion.5
  85.3 13.0 %all-to-all-done.1 = f32[16,2,4096]{2,1,0:T(2,128)S(1)} async-done(((f32[16,2,4096]{2,1,0:T(2,128)}), f32[16,2,4096]{2,1,0:T(2,128)S(1)}, u32[]{:S(2)}, u32[]{:S(2)}) %all-to-all-start.1) | async-done | bytes 524320 | tf_op jit(solution)/shard_map/all_to_all | solution.py:169
  98.3 0.3 copy.27
  98.6 0.1 reshape.313
  98.7 2.0 %convolution_bitcast_fusion.4 = f32[2,256,256]{1,2,0:T(8,128)S(1)} fusion(f32[2,256,256]{2,1,0:T(8,128)S(1)} %reshape.313, f32[256]{0:T(256)S(1)} %fusion.88, s32[256]{0:T(256)S(1)} %iota_select_fusion, pred[256]{0:T(512)(128)(4,1)S(1)} %iota_compare_fusion.5), kind=kOutput, calls=%fused_computation.27 | convolution fusion | flops 403701760 | bytes 1050880 | tf_op jit(solution)/shard_map/ab,...bx->...ax/dot_general | solution.py:77
  100.7 2.0 %fusion.31 = f32[2,256,256]{2,1,0:T(8,128)S(1)} fusion(f32[2,256,256]{1,2,0:T(8,128)S(1)} %convolution_bitcast_fusion.4, f32[256]{0:T(256)S(1)} %fusion.88, s32[256]{0:T(256)S(1)} %iota_select_fusion, pred[256]{0:T(512)(128)(4,1)S(1)} %iota_compare_fusion.5), kind=kOutput, calls=%fused_computation.68 | convolution fusion | flops 403701760 | bytes 1050880 | tf_op jit(solution)/shard_map/...yb,ab->...ya/dot_general | solution.py:73
  102.8 0.0 copy-start.3
  102.8 2.4 %collective-permute-start.3 = (f32[1,256,256]{2,1,0:T(8,128)S(1)}, f32[1,256,256]{2,1,0:T(8,128)S(1)}, u32[]{:S(2)}, u32[]{:S(2)}) collective-permute-start(f32[1,256,256]{2,1,0:T(8,128)S(1)} %get-tuple-element.6), channel_id=1, source_target_pairs={{1,0},{2,1},{3,2},{4,3},{5,4},{6,5},{7,6},{8,7},{9,8},{10,9},{11,1... | collective-permute-start | bytes 786440 | tf_op jit(solution)/shard_map/ppermute | solution.py:33
  105.2 0.6 convolution_bitcast_fusion.2
  105.9 0.6 convolution_bitcast_fusion.3
  106.5 4.0 %collective-permute-done.3 = f32[1,256,256]{2,1,0:T(8,128)S(1)} collective-permute-done((f32[1,256,256]{2,1,0:T(8,128)S(1)}, f32[1,256,256]{2,1,0:T(8,128)S(1)}, u32[]{:S(2)}, u32[]{:S(2)}) %collective-permute-start.3) | collective-permute-done | bytes 262176 | tf_op jit(solution)/shard_map/ppermute | solution.py:33
  110.5 0.1 fusion.23
  110.6 1.4 %maximum_subtract_fusion = f32[1,3,2,256,256]{4,3,2,1,0:T(8,128)} fusion(f32[1,1,2,256,256]{4,3,2,1,0:T(8,128)S(1)} %slice_bitcast_fusion.5, f32[1,2,2,256,256]{4,3,2,1,0:T(8,128)S(1)} %bitcast.116, f32[1,1,2,256,256]{4,3,2,1,0:T(8,128)S(1)} %fusion.23, f32[1,1,2,256,256]{4,3,2,1,0:T(8,128)S(1)} %convolution_bitcast_fusion.2, ...), kind=kLoop, calls=%fused_computation.24 | loop fusion | flops 1572864 | bytes 4718592 | tf_op jit(solution)/shard_map/sub | solution.py:176
  (28 shorter events, 0.2 us)
Async XLA Ops:
  0.6 76.8 %copy-start = (f32[32,32]{1,0:T(8,128)S(1)}, f32[32,32]{1,0:T(8,128)}, u32[]{:S(2)}) copy-start(f32[32,32]{1,0:T(8,128)} %param.14) | copy-start | bytes 12292
  0.6 13.9 %copy-start.1 = (f32[1,3,2,256,256]{4,3,2,1,0:T(8,128)S(1)}, f32[1,3,2,256,256]{4,3,2,1,0:T(8,128)}, u32[]{:S(2)}) copy-start(f32[1,3,2,256,256]{4,3,2,1,0:T(8,128)} %param.8) | copy-start | bytes 4718596
  0.7 13.7 %copy-start.6 = (s32[64]{0:T(128)S(1)}, s32[64]{0:T(128)}, u32[]{:S(2)}) copy-start(s32[64]{0:T(128)} %param.10) | copy-start | bytes 772
  0.7 13.8 %copy-start.5 = (s32[64]{0:T(128)S(1)}, s32[64]{0:T(128)}, u32[]{:S(2)}) copy-start(s32[64]{0:T(128)} %param.12) | copy-start | bytes 772
  0.7 13.9 %copy-start.4 = (s32[64]{0:T(128)S(1)}, s32[64]{0:T(128)}, u32[]{:S(2)}) copy-start(s32[64]{0:T(128)} %param.11) | copy-start | bytes 772
  0.7 14.3 %copy-start.7 = (f32[64]{0:T(128)S(1)}, f32[64]{0:T(128)}, u32[]{:S(2)}) copy-start(f32[64]{0:T(128)} %param.13) | copy-start | bytes 772
  0.7 39.2 %collective-permute-start = (f32[3,2,256,256]{3,2,1,0:T(8,128)}, f32[3,2,256,256]{3,2,1,0:T(8,128)S(1)}, u32[]{:S(2)}, u32[]{:S(2)}) collective-permute-start(f32[3,2,256,256]{3,2,1,0:T(8,128)} %bitcast.111), channel_id=1, source_target_pairs={{0,1},{1,2},{2,3},{3,4},{4,5},{5,6},{6,7},{7,8},{8,9},{9,10},{10,1... | collective-permute-start | bytes 4718600 | tf_op jit(solution)/shard_map/ppermute | solution.py:21
  5.4 36.9 %collective-permute-start.1 = (f32[3,2,256,256]{3,2,1,0:T(8,128)}, f32[3,2,256,256]{3,2,1,0:T(8,128)}, u32[]{:S(2)}, u32[]{:S(2)}) collective-permute-start(f32[3,2,256,256]{3,2,1,0:T(8,128)} %bitcast.112), channel_id=1, source_target_pairs={{1,0},{2,1},{3,2},{4,3},{5,4},{6,5},{7,6},{8,7},{9,8},{10,9},{11,1... | collective-permute-start | bytes 4718600 | tf_op jit(solution)/shard_map/ppermute | solution.py:23
  9.6 38.5 %collective-permute-start.2 = (f32[2,2,256,256]{3,2,1,0:T(8,128)}, f32[2,2,256,256]{3,2,1,0:T(8,128)}, u32[]{:S(2)}, u32[]{:S(2)}) collective-permute-start(f32[2,2,256,256]{3,2,1,0:T(8,128)} %slice_bitcast_fusion), channel_id=1, source_target_pairs={{0,16},{1,17},{2,18},{3,19},{4,20},{5,21},{6,22},{7,23},{8,24},{9,... | collective-permute-start | bytes 3145736 | tf_op jit(solution)/shard_map/ppermute | solution.py:33
  48.1 2.7 %copy-start.2 = (f32[3,2,256,256]{3,2,1,0:T(8,128)}, f32[3,2,256,256]{3,2,1,0:T(8,128)S(1)}, u32[]{:S(2)}) copy-start(f32[3,2,256,256]{3,2,1,0:T(8,128)S(1)} %fusion.9) | copy-start | bytes 4718596
  55.7 21.7 %copy-start.8 = (f32[32]{0:T(128)S(1)}, f32[32]{0:T(128)}, u32[]{:S(2)}) copy-start(f32[32]{0:T(128)} %param.15) | copy-start | bytes 388
  56.9 20.2 %all-to-all-start = ((f32[2,16,4096]{2,0,1:T(2,128)}), f32[2,16,4096]{2,0,1:T(2,128)S(1)}, u32[]{:S(2)}, u32[]{:S(2)}) async-start(f32[2,16,4096]{2,0,1:T(2,128)} %copy.26), calls=%async_computation | async-start | bytes 1048576 | tf_op jit(solution)/shard_map/all_to_all | solution.py:161
  79.7 18.6 %all-to-all-start.1 = ((f32[16,2,4096]{2,1,0:T(2,128)}), f32[16,2,4096]{2,1,0:T(2,128)S(1)}, u32[]{:S(2)}, u32[]{:S(2)}) async-start(f32[16,2,4096]{2,1,0:T(2,128)} %all_to_all.30), calls=%async_computation.1 | async-start | bytes 1048576 | tf_op jit(solution)/shard_map/all_to_all | solution.py:169
  102.8 7.8 %copy-start.3 = (f32[2,256,256]{2,1,0:T(8,128)}, f32[2,256,256]{2,1,0:T(8,128)S(1)}, u32[]{:S(2)}) copy-start(f32[2,256,256]{2,1,0:T(8,128)S(1)} %fusion.31) | copy-start | bytes 1572868
  102.8 7.7 %collective-permute-start.3 = (f32[1,256,256]{2,1,0:T(8,128)S(1)}, f32[1,256,256]{2,1,0:T(8,128)S(1)}, u32[]{:S(2)}, u32[]{:S(2)}) collective-permute-start(f32[1,256,256]{2,1,0:T(8,128)S(1)} %get-tuple-element.6), channel_id=1, source_target_pairs={{1,0},{2,1},{3,2},{4,3},{5,4},{6,5},{7,6},{8,7},{9,8},{10,9},{11,1... | collective-permute-start | bytes 786440 | tf_op jit(solution)/shard_map/ppermute | solution.py:33
where the time goes:
time: 113 us; the launch traced here: 112 us
  waiting for transfers between devices  52.5 us (46%)
  starting transfers between devices  23.6 us (21%)
  matrix products  23.2 us (21%)
  local copies, waits for them, and re-layouts  6.71 us (6%)
  other arithmetic  4.24 us (4%)
  between operations  1.7 us (2%)
    ppermute x1, waiting for transfers between devices, padded(): lax.ppermute(tail, axis, [(i, (i + 1) % count) for i in range(ends)])  21.4 us
    all_to_all x1, waiting for transfers between devices, local(): lax.all_to_all(spectrum, 'gz', split_axis=1, concat_axis=0, tiled=True)  14 us
    all_to_all x1, waiting for transfers between devices, local(): lax.all_to_all(pressure_modes, 'gz', split_axis=0, concat_axis=1, tiled=T...  13 us
    dot_general x5, matrix products, y_derivative(): return jnp.einsum('ab,...bx->...ax', matrix, field, precision=highest)  10.3 us
    dot_general x5, matrix products, x_derivative(): return jnp.einsum('...yb,ab->...ya', field, matrix, precision=highest)  7.45 us
    ppermute x2, starting transfers between devices, from_behind(): return lax.ppermute(value, axis, pairs)  6.47 us
    all_to_all x1, starting transfers between devices, local(): lax.all_to_all(spectrum, 'gz', split_axis=1, concat_axis=0, tiled=True)  6.08 us
    ppermute x1, starting transfers between devices, padded(): lax.ppermute(tail, axis, [(i, (i + 1) % count) for i in range(ends)])  4.67 us
  transfers between devices with their start and end apart: 6, of which 4 were waited for; matrix products, arithmetic and copies ran while one was open for 15% of the time, Pallas kernels for 0%

commit v1 on v0

v1 whole, which is shorter than its diff:
```python
import functools

import jax
import jax.numpy as jnp
import numpy as np
from jax import lax
from jax.experimental import pallas as pl
from jax.experimental.pallas import tpu as pltpu
from jax.sharding import PartitionSpec as P

FRINGE = 32
TIME_STEP = 0.25
MESH = pl.DeviceIdType.MESH
F32 = jnp.float32
BF16 = jnp.bfloat16


def tables(length):
    ids = np.arange(length)
    middle = length // 2
    wave = np.where(ids <= middle, ids, ids - middle)
    phases = 2.0 * np.pi / length * ((wave[:, None] * ids[None, :]) % length)
    norm = np.sqrt(np.where((ids == 0) | (ids == middle), 1.0, 2.0) / length)[:, None]
    basis = np.where(ids[:, None] <= middle, np.cos(phases), np.sin(phases)) * norm
    coupling = np.zeros((length, length))
    inner = np.arange(1, middle)
    coupling[inner, inner + middle] = 2.0 * np.pi * inner / length
    coupling[inner + middle, inner] = -2.0 * np.pi * inner / length
    deriv = basis.T @ coupling @ basis
    deriv = 0.5 * (deriv - deriv.T)
    parts = []
    for matrix in (basis, basis.T, deriv):
        whole = matrix.astype(np.float32)
        high = whole.astype(jnp.bfloat16)
        parts += [high, (whole - high.astype(np.float32)).astype(jnp.bfloat16)]
    return np.stack(parts)


def split(value):
    high = value.astype(BF16)
    return high, (value - high.astype(F32)).astype(BF16)


def dot(left, right):
    return jnp.dot(left, right, preferred_element_type=F32)


def dot_nt(left, right):
    return lax.dot_general(left, right, (((1,), (1,)), ((), ())), preferred_element_type=F32)


def left_mul(high, low, value):
    vh, vl = split(value)
    return dot(jnp.concatenate([high, high, low], 1), jnp.concatenate([vh, vl, vh], 0))


def right_mul(value, high, low):
    vh, vl = split(value)
    return dot(jnp.concatenate([vh, vl, vh], 1), jnp.concatenate([high, high, low], 0))


def iota(shape, dim):
    return lax.broadcasted_iota(jnp.int32, shape, dim)


def onehot(hit):
    return jnp.where(hit, 1.0, 0.0).astype(BF16)


def kernel(
    n, groups,
    vel, start_ref, tlevel, trow, tcol, thrust, green, shift, ramp_tab, tab_y, tab_x,
    upd, prs,
    below, above, fr_src, fr_buf, p_above,
    spec, modes, back, planes, m_hi, m_lo, mt_hi, mt_lo, inv,
    halo_send, halo_recv, fr_send, fr_recv, pa_send, pa_recv, x_send, x_recv, y_send, y_recv,
):
    levels, ny, nx = vel.shape[1:]
    rows = ny // n
    nz = levels * n
    nb = nz * rows
    me = lax.axis_index("gz")
    group = lax.axis_index("group")
    up = lax.rem(me + 1, n)
    down = lax.rem(me + n - 1, n)
    top = levels - 1
    has_up = me < n - 1
    has_down = me > 0

    barrier = pltpu.get_barrier_semaphore()

    @pl.loop(1, n)
    def _(off):
        pl.semaphore_signal(
            barrier, inc=1, device_id={"gz": lax.rem(me + off, n)}, device_id_type=MESH
        )

    for off in range(1, groups):
        pl.semaphore_signal(
            barrier, inc=1, device_id={"group": lax.rem(group + off, groups)}, device_id_type=MESH
        )
    pl.semaphore_wait(barrier, n - 1 + groups - 1)

    def remote(src, dst, send, recv, where):
        return pltpu.make_async_remote_copy(
            src_ref=src, dst_ref=dst, send_sem=send, recv_sem=recv,
            device_id=where, device_id_type=MESH,
        )

    w_up = remote(vel.at[2, top], below.at[2], halo_send.at[0], halo_recv.at[0], {"gz": up})
    all_down = remote(vel.at[:, 0], above, halo_send.at[1], halo_recv.at[1], {"gz": down})
    uv_up = remote(
        vel.at[pl.ds(0, 2), top], below.at[pl.ds(0, 2)], halo_send.at[2], halo_recv.at[2],
        {"gz": up},
    )
    w2_up = remote(vel.at[2, top - 1], below.at[3], halo_send.at[3], halo_recv.at[3], {"gz": up})

    @pl.when(has_up)
    def _():
        w_up.start()

    @pl.when(has_down)
    def _():
        all_down.start()

    @pl.when(has_up)
    def _():
        uv_up.start()
        w2_up.start()

    @pl.when(jnp.logical_not(has_down))
    def _():
        below[...] = jnp.zeros_like(below)

    @pl.when(jnp.logical_not(has_up))
    def _():
        above[...] = jnp.zeros_like(above)
        p_above[...] = jnp.zeros_like(p_above)

    start = start_ref[0]
    pick = iota((FRINGE, nx), 1) - start == iota((FRINGE, nx), 0)
    pick_b = onehot(pick)
    fringe_copies = [
        remote(fr_src, fr_buf, fr_send.at[g - 1], fr_recv, {"group": g}) for g in range(1, groups)
    ]

    @pl.when(group == 0)
    def _():
        fr_buf[...] = jnp.zeros_like(fr_buf)
        for c in range(2):
            for k in range(levels):
                vh, vl = split(vel[c, k])
                fr_src[c * levels + k] = dot_nt(pick_b, vh) + dot_nt(pick_b, vl)
        for copy in fringe_copies:
            copy.start()

    is_farm = jnp.where(group > 0, 1.0, 0.0)
    ramp = is_farm * jnp.sum(jnp.where(pick, ramp_tab[...], 0.0), axis=0, keepdims=True)

    r_y = (tab_y[0], tab_y[1])
    rt_y = (tab_y[2], tab_y[3])
    d_y = (tab_y[4], tab_y[5])
    r_x = (tab_x[0], tab_x[1])
    rt_x = (tab_x[2], tab_x[3])
    d_x = (tab_x[4], tab_x[5])

    def dx(value):
        return -right_mul(value, *d_x)

    def dy(value):
        return left_mul(*d_y, value)

    turbines = trow.shape[1]
    pick_row = iota((ny, turbines), 0) == trow[...]
    pick_col = onehot(iota((nx, turbines), 0) == tcol[...])
    speed = jnp.zeros((1, turbines), F32)
    for k in range(levels):
        vh, vl = split(vel[0, k])
        at_col = dot(vh, pick_col) + dot(vl, pick_col)
        here = jnp.sum(jnp.where(pick_row, at_col, 0.0), axis=0, keepdims=True)
        speed = speed + jnp.where(tlevel[...] == me * levels + k, here, 0.0)
    drag = -is_farm * thrust[...] * jnp.abs(speed) * speed
    for k in range(levels):
        for c in range(3):
            field = vel[c, k]
            if k < top and k > 0:
                vertical = vel[c, k + 1] - vel[c, k - 1]
            elif k < top:
                vertical = vel[c, k + 1]
            elif k > 0:
                vertical = -vel[c, k - 1]
            else:
                vertical = jnp.zeros_like(field)
            tend = -(
                vel[0, k] * dx(field) + vel[1, k] * dy(field) + (0.5 * vel[2, k]) * vertical
            )
            if c == 0:
                placed = jnp.where(
                    pick_row & (tlevel[...] == me * levels + k), drag, 0.0
                )
                ph, pw = split(placed)
                tend = tend + dot_nt(ph, pick_col) + dot_nt(pw, pick_col)
            upd[c, k] = field + TIME_STEP * tend

    rbits = rows.bit_length() - 1
    ybits = ny.bit_length() - 1
    eig = iota((nb, nz), 0) >> rbits == iota((nb, nz), 1)
    pos = iota((nb, nz), 0)
    lev = ((pos & (ny - 1)) >> rbits) * levels + (pos >> ybits) == iota((nb, nz), 1)
    eig_b, lev_b = onehot(eig), onehot(lev)
    same = (iota((nb, nb), 0) & (rows - 1)) == (iota((nb, nb), 1) & (rows - 1))
    for part, to, to_t in zip(split(green[...]), (m_hi, m_lo), (mt_hi, mt_lo)):
        wide = dot(eig_b, part).astype(BF16)
        to[...] = jnp.where(same, dot_nt(wide, lev_b), 0.0).astype(BF16)
        wide_t = dot_nt(lev_b, part).astype(BF16)
        to_t[...] = jnp.where(same, dot_nt(wide_t, eig_b), 0.0).astype(BF16)
    shifts = jnp.sum(jnp.where(eig, shift[...], 0.0), axis=1, keepdims=True)

    def wave_square(ids, length):
        wave = jnp.where(ids <= length // 2, ids, ids - length // 2)
        wave = wave.astype(F32) * (2.0 * np.pi / length)
        return wave * wave

    ky = me * rows + (iota((nb, 1), 0) & (rows - 1))
    kx = iota((1, nx), 1)
    inv[...] = 1.0 / (shifts + (wave_square(ky, ny) + wave_square(kx, nx)))

    def put(ref, value):
        if rows % 8 == 0:
            ref[...] = value.reshape(n, rows, nx)
        else:
            for i in range(n):
                ref[i] = value[i * rows : (i + 1) * rows]

    def get(ref):
        if rows % 8 == 0:
            return ref[...].reshape(ny, nx)
        return jnp.concatenate([ref[i] for i in range(n)], 0)

    def exchange(src, dst, send, recv):
        pltpu.make_async_copy(src.at[me], dst.at[me], recv).start()

        @pl.loop(1, n)
        def _(off):
            peer = lax.rem(me + off, n)
            remote(src.at[peer], dst.at[me], send, recv, {"gz": peer}).start()

    def arrived(dst, recv):
        pltpu.make_async_copy(dst, dst, recv).wait()

    def sent(src, send):
        most = src.at[pl.ds(0, n - 1)]
        pltpu.make_async_copy(most, most, send).wait()

    @pl.when(group > 0)
    def _():
        fringe_copies[0].wait_recv()

    def blend(c, k, predicted):
        th, tl = split(fr_buf[c * levels + k].T)
        upstream = dot(th, pick_b) + dot(tl, pick_b)
        return predicted + ramp * (upstream - predicted)

    def transform(k, under):
        divergence = dx(upd[0, k]) + dy(upd[1, k]) + (upd[2, k] - under)
        put(spec.at[k], right_mul(left_mul(*r_y, divergence), *rt_x))
        exchange(spec.at[k], modes.at[k], x_send.at[k], x_recv.at[k])

    half = 0.5 * TIME_STEP

    @pl.when(has_up)
    def _():
        all_down.wait_recv()

    for c in range(3):
        upd[c, top] = upd[c, top] - half * vel[2, top] * above[c]

    @pl.when(has_down)
    def _():
        w_up.wait_recv()

    upd[2, 0] = upd[2, 0] + half * vel[2, 0] * below[2]
    for k in range(top, 0, -1):
        for c in range(2):
            upd[c, k] = blend(c, k, upd[c, k])
        transform(k, upd[2, k - 1])

    @pl.when(has_down)
    def _():
        uv_up.wait_recv()
        w2_up.wait_recv()

    for c in range(2):
        upd[c, 0] = blend(c, 0, upd[c, 0] + half * vel[2, 0] * below[c])
    w_ghost = below[2]
    ghost = w_ghost - TIME_STEP * (
        below[0] * dx(w_ghost)
        + below[1] * dy(w_ghost)
        + (0.5 * w_ghost) * (vel[2, 0] - below[3])
    )
    transform(0, ghost)

    scaled = None
    for k in range(top, -1, -1):
        arrived(modes.at[k], x_recv.at[k])
        cols = pl.ds(k * ny, ny)
        term = left_mul(m_hi[:, cols], m_lo[:, cols], get(modes.at[k]))
        scaled = term if scaled is None else scaled + term
    scaled = scaled * inv[...]
    for k in range(levels):
        own = pl.ds(k * ny, ny)
        put(back.at[k], left_mul(mt_hi[own], mt_lo[own], scaled))
        exchange(back.at[k], planes.at[k], y_send.at[k], y_recv.at[k])

    p_down = remote(prs.at[0], p_above, pa_send, pa_recv, {"gz": down})
    for k in range(levels):
        arrived(planes.at[k], y_recv.at[k])
        pressure = right_mul(left_mul(*rt_y, get(planes.at[k])), *r_x)
        prs[k] = pressure
        if k == 0:

            @pl.when(has_down)
            def _():
                p_down.start()

        else:
            upd[2, k - 1] = upd[2, k - 1] - (pressure - prs[k - 1])
        upd[0, k] = upd[0, k] - dx(pressure)
        upd[1, k] = upd[1, k] - dy(pressure)

    @pl.when(has_up)
    def _():
        p_down.wait_recv()

    upd[2, top] = upd[2, top] - (p_above[...] - prs[top])

    @pl.when(has_up)
    def _():
        w_up.wait_send()
        uv_up.wait_send()
        w2_up.wait_send()

    @pl.when(has_down)
    def _():
        all_down.wait_send()
        p_down.wait_send()

    @pl.when(group == 0)
    def _():
        for copy in fringe_copies:
            copy.wait_send()

    for k in range(levels):
        sent(spec.at[k], x_send.at[k])
        sent(back.at[k], y_send.at[k])


def local(
    n, groups,
    velocity, fringe_start, turbine_level, turbine_row, turbine_col, thrust, green_basis,
    eigen_shift,
):
    _, _, levels, ny, nx = velocity.shape
    rows = ny // n
    nz = levels * n
    nb = nz * rows
    offset = (np.arange(FRINGE) + 0.5)[:, None]
    ramp_tab = (np.sin(np.pi * offset / FRINGE) ** 2).astype(np.float32)
    vmem = pl.BlockSpec(memory_space=pltpu.VMEM)
    smem = pl.BlockSpec(memory_space=pltpu.SMEM)
    plane = (n, rows, nx)
    dma = pltpu.SemaphoreType.DMA
    updated, pressure = pl.pallas_call(
        functools.partial(kernel, n, groups),
        out_shape=(
            jax.ShapeDtypeStruct((3, levels, ny, nx), F32),
            jax.ShapeDtypeStruct((levels, ny, nx), F32),
        ),
        in_specs=[vmem, smem] + [vmem] * 9,
        out_specs=(vmem, vmem),
        scratch_shapes=[
            pltpu.VMEM((4, ny, nx), F32),
            pltpu.VMEM((3, ny, nx), F32),
            pltpu.VMEM((2 * levels, FRINGE, ny), F32),
            pltpu.VMEM((2 * levels, FRINGE, ny), F32),
            pltpu.VMEM((ny, nx), F32),
            pltpu.VMEM((levels, *plane), F32),
            pltpu.VMEM((levels, *plane), F32),
            pltpu.VMEM((levels, *plane), F32),
            pltpu.VMEM((levels, *plane), F32),
            pltpu.VMEM((nb, nb), BF16),
            pltpu.VMEM((nb, nb), BF16),
            pltpu.VMEM((nb, nb), BF16),
            pltpu.VMEM((nb, nb), BF16),
            pltpu.VMEM((nb, nx), F32),
            dma((4,)),
            dma((4,)),
            dma((max(groups - 1, 1),)),
            dma,
            dma,
            dma,
            dma((levels,)),
            dma((levels,)),
            dma((levels,)),
            dma((levels,)),
        ],
        compiler_params=pltpu.CompilerParams(
            collective_id=0, has_side_effects=True, vmem_limit_bytes=44 * 1024 * 1024
        ),
        name="fractional_step",
    )(
        velocity[0], fringe_start,
        turbine_level[None], turbine_row[None], turbine_col[None], thrust[None],
        green_basis, eigen_shift[None], ramp_tab, tables(ny), tables(nx),
    )
    return updated[None], pressure[None]


def solution(mesh):
    return jax.shard_map(
        functools.partial(local, mesh.shape["gz"], mesh.shape["group"]),
        mesh=mesh,
        in_specs=(P("group", None, "gz", None, None), P(), P(), P(), P(), P(), P(), P()),
        out_specs=(P("group", None, "gz", None, None), P("group", "gz", None, None)),
        check_vma=False,
    )
```

time: 113 us -> 65.5 us (0.58)
  the two profiles are of different devices: /device:TPU:1 before, /device:TPU:5 now
where the time goes in v1:
time: 65.5 us; the launch traced here: 65.1 us
  Pallas kernels  54.7 us (84%)
  local copies, waits for them, and re-layouts  9.18 us (14%)
  between operations  1.3 us (2%)
    pallas_call x1, Pallas kernels, local(): pl.pallas_call(functools.partial(kernel, n, groups), out_shape=(jax.Shape...  54.7 us
    unnamed x20, local copies, waits for them, and re-layouts  9.18 us

profile of v1, /device:TPU:5, one launch (start us, length us, event | category | flops | bytes accessed | tf_op | source)
XLA Modules:
  0.0 65.1 jit_solution(8146364182493251321)
XLA Ops:
  1.3 0.0 copy-start
  1.3 1.1 %copy-done = bf16[6,256,256]{2,1,0:T(8,128)(2,1)S(1)} copy-done((bf16[6,256,256]{2,1,0:T(8,128)(2,1)S(1)}, bf16[6,256,256]{2,1,0:T(8,128)(2,1)}, u32[]{:S(2)}) %copy-start) | copy-done | bytes 786456
  2.4 0.0 copy-start.1
  2.4 1.4 %copy-done.1 = f32[1,3,2,256,256]{4,3,2,1,0:T(8,128)S(1)} copy-done((f32[1,3,2,256,256]{4,3,2,1,0:T(8,128)S(1)}, f32[1,3,2,256,256]{4,3,2,1,0:T(8,128)}, u32[]{:S(2)}) %copy-start.1) | copy-done | bytes 1572888
  3.8 0.0 copy-start.2
  3.8 0.7 %copy-done.2 = f32[32,32]{1,0:T(8,128)S(1)} copy-done((f32[32,32]{1,0:T(8,128)S(1)}, f32[32,32]{1,0:T(8,128)}, u32[]{:S(2)}) %copy-start.2) | copy-done | bytes 4120
  4.5 0.0 copy-start.3
  4.5 0.7 %copy-done.3 = f32[32,1]{1,0:T(8,128)S(1)} copy-done((f32[32,1]{1,0:T(8,128)S(1)}, f32[32,1]{1,0:T(8,128)}, u32[]{:S(2)}) %copy-start.3) | copy-done | bytes 152
  5.3 0.0 copy-start.4
  5.3 0.7 %copy-done.4 = s32[64]{0:T(128)S(1)} copy-done((s32[64]{0:T(128)S(1)}, s32[64]{0:T(128)}, u32[]{:S(2)}) %copy-start.4) | copy-done | bytes 280
  5.9 0.0 copy-start.5
  5.9 0.7 %copy-done.5 = s32[64]{0:T(128)S(1)} copy-done((s32[64]{0:T(128)S(1)}, s32[64]{0:T(128)}, u32[]{:S(2)}) %copy-start.5) | copy-done | bytes 280
  6.6 0.0 copy-start.6
  6.6 0.7 %copy-done.6 = s32[64]{0:T(128)S(1)} copy-done((s32[64]{0:T(128)S(1)}, s32[64]{0:T(128)}, u32[]{:S(2)}) %copy-start.6) | copy-done | bytes 280
  7.2 0.0 copy-start.7
  7.2 0.7 %copy-done.7 = f32[64]{0:T(128)S(1)} copy-done((f32[64]{0:T(128)S(1)}, f32[64]{0:T(128)}, u32[]{:S(2)}) %copy-start.7) | copy-done | bytes 280
  7.9 0.0 copy-start.8
  7.9 0.7 %copy-done.8 = f32[32]{0:T(128)S(1)} copy-done((f32[32]{0:T(128)S(1)}, f32[32]{0:T(128)}, u32[]{:S(2)}) %copy-start.8) | copy-done | bytes 152
  8.5 54.7 %fractional_step.1 = (f32[3,2,256,256]{3,2,1,0:T(8,128)S(1)}, f32[2,256,256]{2,1,0:T(8,128)S(1)}) custom-call(f32[3,2,256,256]{3,2,1,0:T(8,128)S(1)} %bitcast.8, s32[1]{0:T(128)S(6)} %copy.15.start_ref, s32[1,64]{1,0:T(1,128)S(1)} %bitcast.11, s32[1,64]{1,0:T(1,128)S(1)} %bitcast.12, s32[1,64]{1,0:T(1,128)S(1)} %bitcast.13, f32[1,64]{1,0:T(1,128)S(1)} %bitcast.14, ...), custom_call_target="tpu_custom_call" | custom-call | tf_op jit(solution)/shard_map/fractional_step/pallas_call | solution.py:373
  63.2 1.1 %copy.16 = f32[1,3,2,256,256]{4,3,2,1,0:T(8,128)} copy(f32[1,3,2,256,256]{4,3,2,1,0:T(8,128)S(1)} %bitcast.9) | data formatting | bytes 3145728
  64.3 0.8 %copy.17 = f32[1,2,256,256]{3,2,1,0:T(8,128)} copy(f32[1,2,256,256]{3,2,1,0:T(8,128)S(1)} %bitcast.10) | data formatting | bytes 1048576
Async XLA Ops:
  1.3 1.1 %copy-start = (bf16[6,256,256]{2,1,0:T(8,128)(2,1)S(1)}, bf16[6,256,256]{2,1,0:T(8,128)(2,1)}, u32[]{:S(2)}) copy-start(bf16[6,256,256]{2,1,0:T(8,128)(2,1)} %constant.5.clone.tab_y.tab_x) | copy-start | bytes 2359300
  2.4 1.4 %copy-start.1 = (f32[1,3,2,256,256]{4,3,2,1,0:T(8,128)S(1)}, f32[1,3,2,256,256]{4,3,2,1,0:T(8,128)}, u32[]{:S(2)}) copy-start(f32[1,3,2,256,256]{4,3,2,1,0:T(8,128)} %param.11) | copy-start | bytes 4718596
  3.8 0.7 %copy-start.2 = (f32[32,32]{1,0:T(8,128)S(1)}, f32[32,32]{1,0:T(8,128)}, u32[]{:S(2)}) copy-start(f32[32,32]{1,0:T(8,128)} %green.1) | copy-start | bytes 12292
  4.5 0.7 %copy-start.3 = (f32[32,1]{1,0:T(8,128)S(1)}, f32[32,1]{1,0:T(8,128)}, u32[]{:S(2)}) copy-start(f32[32,1]{1,0:T(8,128)} %constant.4.clone.ramp_tab) | copy-start | bytes 388
  5.3 0.7 %copy-start.4 = (s32[64]{0:T(128)S(1)}, s32[64]{0:T(128)}, u32[]{:S(2)}) copy-start(s32[64]{0:T(128)} %param.13) | copy-start | bytes 772
  5.9 0.7 %copy-start.5 = (s32[64]{0:T(128)S(1)}, s32[64]{0:T(128)}, u32[]{:S(2)}) copy-start(s32[64]{0:T(128)} %param.14) | copy-start | bytes 772
  6.6 0.7 %copy-start.6 = (s32[64]{0:T(128)S(1)}, s32[64]{0:T(128)}, u32[]{:S(2)}) copy-start(s32[64]{0:T(128)} %param.15) | copy-start | bytes 772
  7.2 0.7 %copy-start.7 = (f32[64]{0:T(128)S(1)}, f32[64]{0:T(128)}, u32[]{:S(2)}) copy-start(f32[64]{0:T(128)} %param.16) | copy-start | bytes 772
  7.9 0.7 %copy-start.8 = (f32[32]{0:T(128)S(1)}, f32[32]{0:T(128)}, u32[]{:S(2)}) copy-start(f32[32]{0:T(128)} %param.18) | copy-start | bytes 388

commit v2 on v1

--- a/solution.py
+++ b/solution.py
@@ -68,13 +68,21 @@
 
 
 def kernel(
-    n, groups,
-    vel, start_ref, tlevel, trow, tcol, thrust, green, shift, ramp_tab, tab_y, tab_x,
-    upd, prs,
-    below, above, fr_src, fr_buf, p_above,
-    spec, modes, back, planes, m_hi, m_lo, mt_hi, mt_lo, inv,
-    halo_send, halo_recv, fr_send, fr_recv, pa_send, pa_recv, x_send, x_recv, y_send, y_recv,
+    n, groups, tab_count,
+    vel_hbm, start_ref, *refs,
 ):
+    staged = refs[: 7 + tab_count]
+    upd_hbm, prs_hbm = refs[7 + tab_count : 9 + tab_count]
+    vel = refs[9 + tab_count]
+    local_refs = refs[10 + tab_count : 17 + 2 * tab_count]
+    tlevel, trow, tcol, thrust, green, shift, ramp_tab = local_refs[:7]
+    tab_y, tab_x = local_refs[7], local_refs[-1]
+    (
+        upd, prs, below, above, h_src, h_below, h_above, fr_src, fr_buf, p_above,
+        spec, modes, back, planes, m_hi, m_lo, mt_hi, mt_lo, inv,
+        in_sem, out_sem, halo_send, halo_recv, fr_send, fr_recv, pa_send, pa_recv,
+        x_send, x_recv, y_send, y_recv,
+    ) = refs[17 + 2 * tab_count :]
     levels, ny, nx = vel.shape[1:]
     rows = ny // n
     nz = levels * n
@@ -87,6 +95,13 @@
     has_up = me < n - 1
     has_down = me > 0
 
+    loads = [
+        pltpu.make_async_copy(src, dst, in_sem.at[i])
+        for i, (src, dst) in enumerate(zip((vel_hbm, *staged), (vel, *local_refs)))
+    ]
+    for load in loads:
+        load.start()
+
     barrier = pltpu.get_barrier_semaphore()
 
     @pl.loop(1, n)
@@ -107,35 +122,55 @@
             device_id=where, device_id_type=MESH,
         )
 
-    w_up = remote(vel.at[2, top], below.at[2], halo_send.at[0], halo_recv.at[0], {"gz": up})
-    all_down = remote(vel.at[:, 0], above, halo_send.at[1], halo_recv.at[1], {"gz": down})
-    uv_up = remote(
-        vel.at[pl.ds(0, 2), top], below.at[pl.ds(0, 2)], halo_send.at[2], halo_recv.at[2],
-        {"gz": up},
-    )
-    w2_up = remote(vel.at[2, top - 1], below.at[3], halo_send.at[3], halo_recv.at[3], {"gz": up})
-
-    @pl.when(has_up)
-    def _():
-        w_up.start()
-
-    @pl.when(has_down)
-    def _():
-        all_down.start()
-
-    @pl.when(has_up)
-    def _():
-        uv_up.start()
-        w2_up.start()
+    def halo(src, dst, i, where):
+        return remote(src, dst, halo_send.at[i], halo_recv.at[i], {"gz": where})
+
+    uv = pl.ds(0, 2)
+    w_up = halo(vel_hbm.at[2, top], below.at[2], 0, up)
+    w_down = halo(vel_hbm.at[2, 0], above.at[2], 1, down)
+    h_up = halo(h_src.at[0], h_below, 2, up)
+    h_down = halo(h_src.at[1], h_above, 3, down)
+    uv_up = halo(vel_hbm.at[uv, top], below.at[uv], 4, up)
+    uv_down = halo(vel_hbm.at[uv, 0], above.at[uv], 5, down)
+
+    def go_up(*copies):
+        @pl.when(has_up)
+        def _():
+            for copy in copies:
+                copy.start()
+
+    def go_down(*copies):
+        @pl.when(has_down)
+        def _():
+            for copy in copies:
+                copy.start()
+
+    def from_below(copy):
+        @pl.when(has_down)
+        def _():
+            copy.wait_recv()
+
+    def from_above(copy):
+        @pl.when(has_up)
+        def _():
+            copy.wait_recv()
+
+    go_up(w_up)
+    go_down(w_down)
 
     @pl.when(jnp.logical_not(has_down))
     def _():
         below[...] = jnp.zeros_like(below)
+        h_below[...] = jnp.zeros_like(h_below)
 
     @pl.when(jnp.logical_not(has_up))
     def _():
         above[...] = jnp.zeros_like(above)
+        h_above[...] = jnp.zeros_like(h_above)
         p_above[...] = jnp.zeros_like(p_above)
+
+    for load in loads:
+        load.wait()
 
     start = start_ref[0]
     pick = iota((FRINGE, nx), 1) - start == iota((FRINGE, nx), 0)
@@ -156,6 +191,7 @@
 
     is_farm = jnp.where(group > 0, 1.0, 0.0)
     ramp = is_farm * jnp.sum(jnp.where(pick, ramp_tab[...], 0.0), axis=0, keepdims=True)
+    keep = 1.0 - ramp
 
     r_y = (tab_y[0], tab_y[1])
     rt_y = (tab_y[2], tab_y[3])
@@ -173,34 +209,66 @@
     turbines = trow.shape[1]
     pick_row = iota((ny, turbines), 0) == trow[...]
     pick_col = onehot(iota((nx, turbines), 0) == tcol[...])
+
+    def predict(c, k):
+        field = vel[c, k]
+        if k < top and k > 0:
+            vertical = vel[c, k + 1] - vel[c, k - 1]
+        elif k < top:
+            vertical = vel[c, k + 1]
+        elif k > 0:
+            vertical = -vel[c, k - 1]
+        else:
+            vertical = jnp.zeros_like(field)
+        tend = -(vel[0, k] * dx(field) + vel[1, k] * dy(field) + (0.5 * vel[2, k]) * vertical)
+        upd[c, k] = field + TIME_STEP * tend
+
+    for k in range(levels):
+        predict(2, k)
+
+    half = 0.5 * TIME_STEP
+
+    from_above(w_down)
+    upd[2, top] = upd[2, top] - half * vel[2, top] * above[2]
+    weight = (half * keep) * above[2]
+    h_src[0] = dx(weight * vel[0, top]) + dy(weight * vel[1, top]) - upd[2, top]
+    go_up(h_up)
+    from_below(w_up)
+    weight = (-half * keep) * below[2]
+    h_src[1] = dx(weight * vel[0, 0]) + dy(weight * vel[1, 0])
+    go_down(h_down)
+    upd[2, 0] = upd[2, 0] + half * vel[2, 0] * below[2]
+
     speed = jnp.zeros((1, turbines), F32)
     for k in range(levels):
         vh, vl = split(vel[0, k])
         at_col = dot(vh, pick_col) + dot(vl, pick_col)
         here = jnp.sum(jnp.where(pick_row, at_col, 0.0), axis=0, keepdims=True)
         speed = speed + jnp.where(tlevel[...] == me * levels + k, here, 0.0)
-    drag = -is_farm * thrust[...] * jnp.abs(speed) * speed
-    for k in range(levels):
-        for c in range(3):
-            field = vel[c, k]
-            if k < top and k > 0:
-                vertical = vel[c, k + 1] - vel[c, k - 1]
-            elif k < top:
-                vertical = vel[c, k + 1]
-            elif k > 0:
-                vertical = -vel[c, k - 1]
-            else:
-                vertical = jnp.zeros_like(field)
-            tend = -(
-                vel[0, k] * dx(field) + vel[1, k] * dy(field) + (0.5 * vel[2, k]) * vertical
-            )
-            if c == 0:
-                placed = jnp.where(
-                    pick_row & (tlevel[...] == me * levels + k), drag, 0.0
-                )
-                ph, pw = split(placed)
-                tend = tend + dot_nt(ph, pick_col) + dot_nt(pw, pick_col)
-            upd[c, k] = field + TIME_STEP * tend
+    drag = (-TIME_STEP * is_farm) * thrust[...] * jnp.abs(speed) * speed
+    for k in range(levels):
+        predict(0, k)
+        placed = jnp.where(pick_row & (tlevel[...] == me * levels + k), drag, 0.0)
+        ph, pw = split(placed)
+        upd[0, k] = upd[0, k] + dot_nt(ph, pick_col) + dot_nt(pw, pick_col)
+        predict(1, k)
+
+    @pl.when(group > 0)
+    def _():
+        fringe_copies[0].wait_recv()
+
+    for k in range(levels):
+        for c in range(2):
+            th, tl = split(fr_buf[c * levels + k].T)
+            upstream = dot(th, pick_b) + dot(tl, pick_b)
+            predicted = upd[c, k]
+            upd[c, k] = predicted + ramp * (upstream - predicted)
+
+    for k in range(levels):
+        divergence = dx(upd[0, k]) + dy(upd[1, k]) + upd[2, k]
+        if k > 0:
+            divergence = divergence - upd[2, k - 1]
+        prs[k] = divergence
 
     rbits = rows.bit_length() - 1
     ybits = ny.bit_length() - 1
@@ -225,18 +293,6 @@
     kx = iota((1, nx), 1)
     inv[...] = 1.0 / (shifts + (wave_square(ky, ny) + wave_square(kx, nx)))
 
-    def put(ref, value):
-        if rows % 8 == 0:
-            ref[...] = value.reshape(n, rows, nx)
-        else:
-            for i in range(n):
-                ref[i] = value[i * rows : (i + 1) * rows]
-
-    def get(ref):
-        if rows % 8 == 0:
-            return ref[...].reshape(ny, nx)
-        return jnp.concatenate([ref[i] for i in range(n)], 0)
-
     def exchange(src, dst, send, recv):
         pltpu.make_async_copy(src.at[me], dst.at[me], recv).start()
 
@@ -252,53 +308,20 @@
         most = src.at[pl.ds(0, n - 1)]
         pltpu.make_async_copy(most, most, send).wait()
 
-    @pl.when(group > 0)
-    def _():
-        fringe_copies[0].wait_recv()
-
-    def blend(c, k, predicted):
-        th, tl = split(fr_buf[c * levels + k].T)
-        upstream = dot(th, pick_b) + dot(tl, pick_b)
-        return predicted + ramp * (upstream - predicted)
-
-    def transform(k, under):
-        divergence = dx(upd[0, k]) + dy(upd[1, k]) + (upd[2, k] - under)
-        put(spec.at[k], right_mul(left_mul(*r_y, divergence), *rt_x))
+    def transform(k):
+        put(spec.at[k], right_mul(left_mul(*r_y, prs[k]), *rt_x), n)
         exchange(spec.at[k], modes.at[k], x_send.at[k], x_recv.at[k])
 
-    half = 0.5 * TIME_STEP
-
-    @pl.when(has_up)
-    def _():
-        all_down.wait_recv()
-
-    for c in range(3):
-        upd[c, top] = upd[c, top] - half * vel[2, top] * above[c]
-
-    @pl.when(has_down)
-    def _():
-        w_up.wait_recv()
-
-    upd[2, 0] = upd[2, 0] + half * vel[2, 0] * below[2]
-    for k in range(top, 0, -1):
-        for c in range(2):
-            upd[c, k] = blend(c, k, upd[c, k])
-        transform(k, upd[2, k - 1])
-
-    @pl.when(has_down)
-    def _():
-        uv_up.wait_recv()
-        w2_up.wait_recv()
-
-    for c in range(2):
-        upd[c, 0] = blend(c, 0, upd[c, 0] + half * vel[2, 0] * below[c])
-    w_ghost = below[2]
-    ghost = w_ghost - TIME_STEP * (
-        below[0] * dx(w_ghost)
-        + below[1] * dy(w_ghost)
-        + (0.5 * w_ghost) * (vel[2, 0] - below[3])
-    )
-    transform(0, ghost)
+    from_above(h_down)
+    prs[top] = prs[top] + h_above[...]
+    if top > 0:
+        transform(top)
+    for k in range(top - 1, 0, -1):
+        transform(k)
+    from_below(h_up)
+    prs[0] = prs[0] + h_below[...]
+    transform(0)
+    go_up(uv_up)
 
     scaled = None
     for k in range(top, -1, -1):
@@ -309,41 +332,52 @@
     scaled = scaled * inv[...]
     for k in range(levels):
         own = pl.ds(k * ny, ny)
-        put(back.at[k], left_mul(mt_hi[own], mt_lo[own], scaled))
+        put(back.at[k], left_mul(mt_hi[own], mt_lo[own], scaled), n)
         exchange(back.at[k], planes.at[k], y_send.at[k], y_recv.at[k])
+    go_down(uv_down)
+
+    from_below(uv_up)
+    for c in range(2):
+        upd[c, 0] = upd[c, 0] + (half * keep) * (vel[2, 0] * below[c])
 
     p_down = remote(prs.at[0], p_above, pa_send, pa_recv, {"gz": down})
+    outs = []
+
+    def leave(src, dst):
+        copy = pltpu.make_async_copy(src, dst, out_sem.at[len(outs)])
+        copy.start()
+        outs.append(copy)
+
     for k in range(levels):
         arrived(planes.at[k], y_recv.at[k])
         pressure = right_mul(left_mul(*rt_y, get(planes.at[k])), *r_x)
         prs[k] = pressure
+        leave(prs.at[k], prs_hbm.at[k])
         if k == 0:
-
-            @pl.when(has_down)
-            def _():
-                p_down.start()
-
+            go_down(p_down)
         else:
             upd[2, k - 1] = upd[2, k - 1] - (pressure - prs[k - 1])
+            leave(upd.at[2, k - 1], upd_hbm.at[2, k - 1])
+        if k == top:
+            from_above(uv_down)
+            for c in range(2):
+                upd[c, top] = upd[c, top] - (half * keep) * (vel[2, top] * above[c])
         upd[0, k] = upd[0, k] - dx(pressure)
         upd[1, k] = upd[1, k] - dy(pressure)
+        leave(upd.at[uv, k], upd_hbm.at[uv, k])
+    from_above(p_down)
+    upd[2, top] = upd[2, top] - (p_above[...] - prs[top])
+    leave(upd.at[2, top], upd_hbm.at[2, top])
 
     @pl.when(has_up)
     def _():
-        p_down.wait_recv()
-
-    upd[2, top] = upd[2, top] - (p_above[...] - prs[top])
-
-    @pl.when(has_up)
-    def _():
-        w_up.wait_send()
-        uv_up.wait_send()
-        w2_up.wait_send()
+        for copy in (w_up, h_up, uv_up):
+            copy.wait_send()
 
     @pl.when(has_down)
     def _():
-        all_down.wait_send()
-        p_down.wait_send()
+        for copy in (w_down, h_down, uv_down, p_down):
+            copy.wait_send()
 
     @pl.when(group == 0)
     def _():
@@ -353,6 +387,24 @@
     for k in range(levels):
         sent(spec.at[k], x_send.at[k])
         sent(back.at[k], y_send.at[k])
+    for copy in outs:
+        copy.wait()
+
+
+def put(ref, value, n):
+    rows = ref.shape[1]
+    if rows % 8 == 0:
+        ref[...] = value.reshape(ref.shape)
+    else:
+        for i in range(n):
+            ref[i] = value[i * rows : (i + 1) * rows]
+
+
+def get(ref):
+    n, rows, nx = ref.shape
+    if rows % 8 == 0:
+        return ref[...].reshape(n * rows, nx)
+    return jnp.concatenate([ref[i] for i in range(n)], 0)
 
 
 def local(
@@ -366,21 +418,33 @@
     nb = nz * rows
     offset = (np.arange(FRINGE) + 0.5)[:, None]
     ramp_tab = (np.sin(np.pi * offset / FRINGE) ** 2).astype(np.float32)
-    vmem = pl.BlockSpec(memory_space=pltpu.VMEM)
+    hbm = pl.BlockSpec(memory_space=pltpu.HBM)
     smem = pl.BlockSpec(memory_space=pltpu.SMEM)
     plane = (n, rows, nx)
     dma = pltpu.SemaphoreType.DMA
+    tabs = [tables(length) for length in ((ny,) if ny == nx else (ny, nx))]
+    staged = [
+        turbine_level[None], turbine_row[None], turbine_col[None], thrust[None],
+        green_basis, eigen_shift[None], ramp_tab, *tabs,
+    ]
+    fields = velocity[0]
     updated, pressure = pl.pallas_call(
-        functools.partial(kernel, n, groups),
+        functools.partial(kernel, n, groups, len(tabs)),
         out_shape=(
             jax.ShapeDtypeStruct((3, levels, ny, nx), F32),
             jax.ShapeDtypeStruct((levels, ny, nx), F32),
         ),
-        in_specs=[vmem, smem] + [vmem] * 9,
-        out_specs=(vmem, vmem),
-        scratch_shapes=[
-            pltpu.VMEM((4, ny, nx), F32),
+        in_specs=[hbm, smem] + [hbm] * len(staged),
+        out_specs=(hbm, hbm),
+        scratch_shapes=[pltpu.VMEM(x.shape, x.dtype) for x in (fields, *staged)]
+        + [
+            pltpu.VMEM((3, levels, ny, nx), F32),
+            pltpu.VMEM((levels, ny, nx), F32),
             pltpu.VMEM((3, ny, nx), F32),
+            pltpu.VMEM((3, ny, nx), F32),
+            pltpu.VMEM((2, ny, nx), F32),
+            pltpu.VMEM((ny, nx), F32),
+            pltpu.VMEM((ny, nx), F32),
             pltpu.VMEM((2 * levels, FRINGE, ny), F32),
             pltpu.VMEM((2 * levels, FRINGE, ny), F32),
             pltpu.VMEM((ny, nx), F32),
@@ -393,8 +457,10 @@
             pltpu.VMEM((nb, nb), BF16),
             pltpu.VMEM((nb, nb), BF16),
             pltpu.VMEM((nb, nx), F32),
-            dma((4,)),
-            dma((4,)),
+            dma((1 + len(staged),)),
+            dma((3 * levels,)),
+            dma((6,)),
+            dma((6,)),
             dma((max(groups - 1, 1),)),
             dma,
             dma,
@@ -405,14 +471,10 @@
             dma((levels,)),
         ],
         compiler_params=pltpu.CompilerParams(
-            collective_id=0, has_side_effects=True, vmem_limit_bytes=44 * 1024 * 1024
+            collective_id=0, has_side_effects=True, vmem_limit_bytes=56 * 1024 * 1024
         ),
         name="fractional_step",
-    )(
-        velocity[0], fringe_start,
-        turbine_level[None], turbine_row[None], turbine_col[None], thrust[None],
-        green_basis, eigen_shift[None], ramp_tab, tables(ny), tables(nx),
-    )
+    )(fields, fringe_start, *staged)
     return updated[None], pressure[None]
 
 

time: 65.5 us -> 57.1 us (0.87)
  the two profiles are of different devices: /device:TPU:5 before, /device:TPU:13 now
where the time goes in v2:
time: 57.1 us; the launch traced here: 56.9 us
  Pallas kernels  52.1 us (91%)
  local copies, waits for them, and re-layouts  3.59 us (6%)
  between operations  1.29 us (2%)
    pallas_call x1, Pallas kernels, local(): pl.pallas_call(functools.partial(kernel, n, groups, len(tabs)), out_shape...  52.1 us
    unnamed x4, local copies, waits for them, and re-layouts  3.59 us

profile of v2, /device:TPU:13, one launch (start us, length us, event | category | flops | bytes accessed | tf_op | source)
XLA Modules:
  0.0 56.9 jit_solution(9957859967456092752)
XLA Ops:
  1.3 52.1 %fractional_step.1 = (f32[3,2,256,256]{3,2,1,0:T(8,128)}, f32[2,256,256]{2,1,0:T(8,128)}) custom-call(f32[3,2,256,256]{3,2,1,0:T(8,128)} %bitcast.8, s32[1]{0:T(128)S(6)} %copy.14.start_ref, s32[1,64]{1,0:T(1,128)} %bitcast.11, s32[1,64]{1,0:T(1,128)} %bitcast.12, s32[1,64]{1,0:T(1,128)} %bitcast.13, f32[1,64]{1,0:T(1,128)} %bitcast.14, f32[32,32]{1,0:T(8,128)} %refs_4_.1, ...), custom_call_target="tpu_custom_call" | custom-call | tf_op jit(solution)/shard_map/fractional_step/pallas_call | solution.py:431
  53.3 0.0 copy-start
  53.4 2.8 %copy.15 = f32[1,3,2,256,256]{4,3,2,1,0:T(8,128)} copy(f32[1,3,2,256,256]{4,3,2,1,0:T(8,128)} %bitcast.9) | data formatting | bytes 3145728
  56.1 0.0 copy-done
  56.2 0.8 %copy.16 = f32[1,2,256,256]{3,2,1,0:T(8,128)} copy(f32[1,2,256,256]{3,2,1,0:T(8,128)S(1)} %bitcast.10) | data formatting | bytes 1048576
Async XLA Ops:
  53.3 2.8 %copy-start = (f32[2,256,256]{2,1,0:T(8,128)S(1)}, f32[2,256,256]{2,1,0:T(8,128)}, u32[]{:S(2)}) copy-start(f32[2,256,256]{2,1,0:T(8,128)} %get-tuple-element.5) | copy-start | bytes 1572868

commit v3 on v2

--- a/solution.py
+++ b/solution.py
@@ -72,15 +72,15 @@
     vel_hbm, start_ref, *refs,
 ):
     staged = refs[: 7 + tab_count]
-    upd_hbm, prs_hbm = refs[7 + tab_count : 9 + tab_count]
+    upd, prs = refs[7 + tab_count : 9 + tab_count]
     vel = refs[9 + tab_count]
     local_refs = refs[10 + tab_count : 17 + 2 * tab_count]
     tlevel, trow, tcol, thrust, green, shift, ramp_tab = local_refs[:7]
     tab_y, tab_x = local_refs[7], local_refs[-1]
     (
-        upd, prs, below, above, h_src, h_below, h_above, fr_src, fr_buf, p_above,
+        w_side, uv_side, h_src, h_side, fr_src, fr_buf, p_above,
         spec, modes, back, planes, m_hi, m_lo, mt_hi, mt_lo, inv,
-        in_sem, out_sem, halo_send, halo_recv, fr_send, fr_recv, pa_send, pa_recv,
+        in_sem, halo_send, halo_recv, fr_send, fr_recv, pa_send, pa_recv,
         x_send, x_recv, y_send, y_recv,
     ) = refs[17 + 2 * tab_count :]
     levels, ny, nx = vel.shape[1:]
@@ -92,8 +92,6 @@
     up = lax.rem(me + 1, n)
     down = lax.rem(me + n - 1, n)
     top = levels - 1
-    has_up = me < n - 1
-    has_down = me > 0
 
     loads = [
         pltpu.make_async_copy(src, dst, in_sem.at[i])
@@ -122,52 +120,52 @@
             device_id=where, device_id_type=MESH,
         )
 
-    def halo(src, dst, i, where):
-        return remote(src, dst, halo_send.at[i], halo_recv.at[i], {"gz": where})
+    inner = 1 - lax.rem(me, 2)
+    outer = 1 - inner
+
+    def there(side):
+        return jnp.where(side == 1, me < n - 1, me > 0)
+
+    def toward(side):
+        return jnp.where(side == 1, up, down)
 
     uv = pl.ds(0, 2)
-    w_up = halo(vel_hbm.at[2, top], below.at[2], 0, up)
-    w_down = halo(vel_hbm.at[2, 0], above.at[2], 1, down)
-    h_up = halo(h_src.at[0], h_below, 2, up)
-    h_down = halo(h_src.at[1], h_above, 3, down)
-    uv_up = halo(vel_hbm.at[uv, top], below.at[uv], 4, up)
-    uv_down = halo(vel_hbm.at[uv, 0], above.at[uv], 5, down)
-
-    def go_up(*copies):
-        @pl.when(has_up)
+
+    def halo(src, dst, kind, side):
+        return remote(
+            src, dst.at[1 - side], halo_send.at[kind, side], halo_recv.at[kind, 1 - side],
+            {"gz": toward(side)},
+        )
+
+    def halo_copy(kind, side):
+        if kind == 0:
+            return halo(vel_hbm.at[2, side * top], w_side, kind, side)
+        if kind == 1:
+            return halo(h_src.at[side], h_side, kind, side)
+        return halo(vel_hbm.at[uv, side * top], uv_side, kind, side)
+
+    def send(kind, side):
+        @pl.when(there(side))
         def _():
-            for copy in copies:
-                copy.start()
-
-    def go_down(*copies):
-        @pl.when(has_down)
+            halo_copy(kind, side).start()
+
+    def receive(kind, side):
+        @pl.when(there(side))
         def _():
-            for copy in copies:
-                copy.start()
-
-    def from_below(copy):
-        @pl.when(has_down)
+            halo_copy(kind, 1 - side).wait_recv()
+
+    send(0, inner)
+    send(0, outer)
+
+    for side in range(2):
+
+        @pl.when(jnp.logical_not(there(side)))
         def _():
-            copy.wait_recv()
-
-    def from_above(copy):
-        @pl.when(has_up)
-        def _():
-            copy.wait_recv()
-
-    go_up(w_up)
-    go_down(w_down)
-
-    @pl.when(jnp.logical_not(has_down))
-    def _():
-        below[...] = jnp.zeros_like(below)
-        h_below[...] = jnp.zeros_like(h_below)
-
-    @pl.when(jnp.logical_not(has_up))
-    def _():
-        above[...] = jnp.zeros_like(above)
-        h_above[...] = jnp.zeros_like(h_above)
-        p_above[...] = jnp.zeros_like(p_above)
+            w_side[side] = jnp.zeros((ny, nx), F32)
+            h_side[side] = jnp.zeros((ny, nx), F32)
+            uv_side[side] = jnp.zeros((2, ny, nx), F32)
+            if side == 1:
+                p_above[...] = jnp.zeros((ny, nx), F32)
 
     for load in loads:
         load.wait()
@@ -228,16 +226,19 @@
 
     half = 0.5 * TIME_STEP
 
-    from_above(w_down)
-    upd[2, top] = upd[2, top] - half * vel[2, top] * above[2]
-    weight = (half * keep) * above[2]
-    h_src[0] = dx(weight * vel[0, top]) + dy(weight * vel[1, top]) - upd[2, top]
-    go_up(h_up)
-    from_below(w_up)
-    weight = (-half * keep) * below[2]
-    h_src[1] = dx(weight * vel[0, 0]) + dy(weight * vel[1, 0])
-    go_down(h_down)
-    upd[2, 0] = upd[2, 0] + half * vel[2, 0] * below[2]
+    for side in (inner, outer):
+        signed = half * (2 * side - 1).astype(F32)
+        edge = side * top
+        receive(0, side)
+        w_there = w_side[side]
+        upd[2, edge] = upd[2, edge] - signed * (vel[2, edge] * w_there)
+        weight = (signed * keep) * w_there
+        h_src[side] = (
+            dx(weight * vel[0, edge])
+            + dy(weight * vel[1, edge])
+            - side.astype(F32) * upd[2, top]
+        )
+        send(1, side)
 
     speed = jnp.zeros((1, turbines), F32)
     for k in range(levels):
@@ -312,16 +313,14 @@
         put(spec.at[k], right_mul(left_mul(*r_y, prs[k]), *rt_x), n)
         exchange(spec.at[k], modes.at[k], x_send.at[k], x_recv.at[k])
 
-    from_above(h_down)
-    prs[top] = prs[top] + h_above[...]
-    if top > 0:
-        transform(top)
-    for k in range(top - 1, 0, -1):
+    for side in (inner, outer):
+        edge = side * top
+        receive(1, side)
+        prs[edge] = prs[edge] + h_side[side]
+        transform(edge)
+    for k in range(1, top):
         transform(k)
-    from_below(h_up)
-    prs[0] = prs[0] + h_below[...]
-    transform(0)
-    go_up(uv_up)
+    send(2, 1)
 
     scaled = None
     for k in range(top, -1, -1):
@@ -334,50 +333,48 @@
         own = pl.ds(k * ny, ny)
         put(back.at[k], left_mul(mt_hi[own], mt_lo[own], scaled), n)
         exchange(back.at[k], planes.at[k], y_send.at[k], y_recv.at[k])
-    go_down(uv_down)
-
-    from_below(uv_up)
+    send(2, 0)
+
+    receive(2, 0)
     for c in range(2):
-        upd[c, 0] = upd[c, 0] + (half * keep) * (vel[2, 0] * below[c])
+        upd[c, 0] = upd[c, 0] + (half * keep) * (vel[2, 0] * uv_side[0, c])
 
     p_down = remote(prs.at[0], p_above, pa_send, pa_recv, {"gz": down})
-    outs = []
-
-    def leave(src, dst):
-        copy = pltpu.make_async_copy(src, dst, out_sem.at[len(outs)])
-        copy.start()
-        outs.append(copy)
 
     for k in range(levels):
         arrived(planes.at[k], y_recv.at[k])
         pressure = right_mul(left_mul(*rt_y, get(planes.at[k])), *r_x)
         prs[k] = pressure
-        leave(prs.at[k], prs_hbm.at[k])
         if k == 0:
-            go_down(p_down)
+            @pl.when(there(0))
+            def _():
+                p_down.start()
+
         else:
             upd[2, k - 1] = upd[2, k - 1] - (pressure - prs[k - 1])
-            leave(upd.at[2, k - 1], upd_hbm.at[2, k - 1])
         if k == top:
-            from_above(uv_down)
+            receive(2, 1)
             for c in range(2):
-                upd[c, top] = upd[c, top] - (half * keep) * (vel[2, top] * above[c])
+                upd[c, top] = upd[c, top] - (half * keep) * (vel[2, top] * uv_side[1, c])
         upd[0, k] = upd[0, k] - dx(pressure)
         upd[1, k] = upd[1, k] - dy(pressure)
-        leave(upd.at[uv, k], upd_hbm.at[uv, k])
-    from_above(p_down)
+
+    @pl.when(there(1))
+    def _():
+        p_down.wait_recv()
+
     upd[2, top] = upd[2, top] - (p_above[...] - prs[top])
-    leave(upd.at[2, top], upd_hbm.at[2, top])
-
-    @pl.when(has_up)
+
+    for side in range(2):
+
+        @pl.when(there(side))
+        def _():
+            for kind in range(3):
+                halo_copy(kind, side).wait_send()
+
+    @pl.when(there(0))
     def _():
-        for copy in (w_up, h_up, uv_up):
-            copy.wait_send()
-
-    @pl.when(has_down)
-    def _():
-        for copy in (w_down, h_down, uv_down, p_down):
-            copy.wait_send()
+        p_down.wait_send()
 
     @pl.when(group == 0)
     def _():
@@ -387,8 +384,6 @@
     for k in range(levels):
         sent(spec.at[k], x_send.at[k])
         sent(back.at[k], y_send.at[k])
-    for copy in outs:
-        copy.wait()
 
 
 def put(ref, value, n):
@@ -419,6 +414,7 @@
     offset = (np.arange(FRINGE) + 0.5)[:, None]
     ramp_tab = (np.sin(np.pi * offset / FRINGE) ** 2).astype(np.float32)
     hbm = pl.BlockSpec(memory_space=pltpu.HBM)
+    vmem = pl.BlockSpec(memory_space=pltpu.VMEM)
     smem = pl.BlockSpec(memory_space=pltpu.SMEM)
     plane = (n, rows, nx)
     dma = pltpu.SemaphoreType.DMA
@@ -435,16 +431,13 @@
             jax.ShapeDtypeStruct((levels, ny, nx), F32),
         ),
         in_specs=[hbm, smem] + [hbm] * len(staged),
-        out_specs=(hbm, hbm),
+        out_specs=(vmem, vmem),
         scratch_shapes=[pltpu.VMEM(x.shape, x.dtype) for x in (fields, *staged)]
         + [
-            pltpu.VMEM((3, levels, ny, nx), F32),
-            pltpu.VMEM((levels, ny, nx), F32),
-            pltpu.VMEM((3, ny, nx), F32),
-            pltpu.VMEM((3, ny, nx), F32),
             pltpu.VMEM((2, ny, nx), F32),
-            pltpu.VMEM((ny, nx), F32),
-            pltpu.VMEM((ny, nx), F32),
+            pltpu.VMEM((2, 2, ny, nx), F32),
+            pltpu.VMEM((2, ny, nx), F32),
+            pltpu.VMEM((2, ny, nx), F32),
             pltpu.VMEM((2 * levels, FRINGE, ny), F32),
             pltpu.VMEM((2 * levels, FRINGE, ny), F32),
             pltpu.VMEM((ny, nx), F32),
@@ -458,9 +451,8 @@
             pltpu.VMEM((nb, nb), BF16),
             pltpu.VMEM((nb, nx), F32),
             dma((1 + len(staged),)),
-            dma((3 * levels,)),
-            dma((6,)),
-            dma((6,)),
+            dma((3, 2)),
+            dma((3, 2)),
             dma((max(groups - 1, 1),)),
             dma,
             dma,
@@ -471,7 +463,7 @@
             dma((levels,)),
         ],
         compiler_params=pltpu.CompilerParams(
-            collective_id=0, has_side_effects=True, vmem_limit_bytes=56 * 1024 * 1024
+            collective_id=0, has_side_effects=True, vmem_limit_bytes=40 * 1024 * 1024
         ),
         name="fractional_step",
     )(fields, fringe_start, *staged)

time: 57.1 us -> 60.2 us (1.054)
  the two profiles are of different devices: /device:TPU:13 before, /device:TPU:15 now
where the time goes in v3:
time: 60.2 us; the launch traced here: 59.8 us
  Pallas kernels  49.3 us (82%)
  local copies, waits for them, and re-layouts  9.18 us (15%)
  between operations  1.3 us (2%)
    pallas_call x1, Pallas kernels, local(): pl.pallas_call(functools.partial(kernel, n, groups, len(tabs)), out_shape...  49.3 us
    unnamed x20, local copies, waits for them, and re-layouts  9.18 us

profile of v3, /device:TPU:15, one launch (start us, length us, event | category | flops | bytes accessed | tf_op | source)
XLA Modules:
  0.0 59.8 jit_solution(3573265336400597481)
XLA Ops:
  1.3 0.0 copy-start
  1.3 1.4 %copy-done = f32[1,3,2,256,256]{4,3,2,1,0:T(8,128)S(1)} copy-done((f32[1,3,2,256,256]{4,3,2,1,0:T(8,128)S(1)}, f32[1,3,2,256,256]{4,3,2,1,0:T(8,128)}, u32[]{:S(2)}) %copy-start) | copy-done | bytes 1572888
  2.7 0.0 copy-start.1
  2.7 1.1 %copy-done.1 = bf16[6,256,256]{2,1,0:T(8,128)(2,1)S(1)} copy-done((bf16[6,256,256]{2,1,0:T(8,128)(2,1)S(1)}, bf16[6,256,256]{2,1,0:T(8,128)(2,1)}, u32[]{:S(2)}) %copy-start.1) | copy-done | bytes 786456
  3.8 0.0 copy-start.2
  3.8 0.7 %copy-done.2 = f32[32,32]{1,0:T(8,128)S(1)} copy-done((f32[32,32]{1,0:T(8,128)S(1)}, f32[32,32]{1,0:T(8,128)}, u32[]{:S(2)}) %copy-start.2) | copy-done | bytes 4120
  4.5 0.0 copy-start.3
  4.5 0.7 %copy-done.3 = f32[32,1]{1,0:T(8,128)S(1)} copy-done((f32[32,1]{1,0:T(8,128)S(1)}, f32[32,1]{1,0:T(8,128)}, u32[]{:S(2)}) %copy-start.3) | copy-done | bytes 152
  5.3 0.0 copy-start.4
  5.3 0.7 %copy-done.4 = s32[64]{0:T(128)S(1)} copy-done((s32[64]{0:T(128)S(1)}, s32[64]{0:T(128)}, u32[]{:S(2)}) %copy-start.4) | copy-done | bytes 280
  5.9 0.0 copy-start.5
  5.9 0.7 %copy-done.5 = s32[64]{0:T(128)S(1)} copy-done((s32[64]{0:T(128)S(1)}, s32[64]{0:T(128)}, u32[]{:S(2)}) %copy-start.5) | copy-done | bytes 280
  6.6 0.0 copy-start.6
  6.6 0.7 %copy-done.6 = s32[64]{0:T(128)S(1)} copy-done((s32[64]{0:T(128)S(1)}, s32[64]{0:T(128)}, u32[]{:S(2)}) %copy-start.6) | copy-done | bytes 280
  7.2 0.0 copy-start.7
  7.2 0.7 %copy-done.7 = f32[64]{0:T(128)S(1)} copy-done((f32[64]{0:T(128)S(1)}, f32[64]{0:T(128)}, u32[]{:S(2)}) %copy-start.7) | copy-done | bytes 280
  7.9 0.0 copy-start.8
  7.9 0.7 %copy-done.8 = f32[32]{0:T(128)S(1)} copy-done((f32[32]{0:T(128)S(1)}, f32[32]{0:T(128)}, u32[]{:S(2)}) %copy-start.8) | copy-done | bytes 152
  8.5 49.3 %fractional_step.1 = (f32[3,2,256,256]{3,2,1,0:T(8,128)S(1)}, f32[2,256,256]{2,1,0:T(8,128)S(1)}) custom-call(f32[3,2,256,256]{3,2,1,0:T(8,128)S(1)} %bitcast.8, s32[1]{0:T(128)S(6)} %copy.14.start_ref, s32[1,64]{1,0:T(1,128)S(1)} %bitcast.11, s32[1,64]{1,0:T(1,128)S(1)} %bitcast.12, s32[1,64]{1,0:T(1,128)S(1)} %bitcast.13, f32[1,64]{1,0:T(1,128)S(1)} %bitcast.14, ...), custom_call_target="tpu_custom_call" | custom-call | tf_op jit(solution)/shard_map/fractional_step/pallas_call | solution.py:427
  57.8 1.1 %copy.15 = f32[1,3,2,256,256]{4,3,2,1,0:T(8,128)} copy(f32[1,3,2,256,256]{4,3,2,1,0:T(8,128)S(1)} %bitcast.9) | data formatting | bytes 3145728
  59.0 0.8 %copy.16 = f32[1,2,256,256]{3,2,1,0:T(8,128)} copy(f32[1,2,256,256]{3,2,1,0:T(8,128)S(1)} %bitcast.10) | data formatting | bytes 1048576
Async XLA Ops:
  1.3 1.4 %copy-start = (f32[1,3,2,256,256]{4,3,2,1,0:T(8,128)S(1)}, f32[1,3,2,256,256]{4,3,2,1,0:T(8,128)}, u32[]{:S(2)}) copy-start(f32[1,3,2,256,256]{4,3,2,1,0:T(8,128)} %param.10) | copy-start | bytes 4718596
  2.7 1.1 %copy-start.1 = (bf16[6,256,256]{2,1,0:T(8,128)(2,1)S(1)}, bf16[6,256,256]{2,1,0:T(8,128)(2,1)}, u32[]{:S(2)}) copy-start(bf16[6,256,256]{2,1,0:T(8,128)(2,1)} %constant.5.clone.refs_7_) | copy-start | bytes 2359300
  3.8 0.7 %copy-start.2 = (f32[32,32]{1,0:T(8,128)S(1)}, f32[32,32]{1,0:T(8,128)}, u32[]{:S(2)}) copy-start(f32[32,32]{1,0:T(8,128)} %refs_4_.1) | copy-start | bytes 12292
  4.5 0.7 %copy-start.3 = (f32[32,1]{1,0:T(8,128)S(1)}, f32[32,1]{1,0:T(8,128)}, u32[]{:S(2)}) copy-start(f32[32,1]{1,0:T(8,128)} %constant.4.clone.refs_6_) | copy-start | bytes 388
  5.3 0.7 %copy-start.4 = (s32[64]{0:T(128)S(1)}, s32[64]{0:T(128)}, u32[]{:S(2)}) copy-start(s32[64]{0:T(128)} %param.12) | copy-start | bytes 772
  5.9 0.7 %copy-start.5 = (s32[64]{0:T(128)S(1)}, s32[64]{0:T(128)}, u32[]{:S(2)}) copy-start(s32[64]{0:T(128)} %param.13) | copy-start | bytes 772
  6.6 0.7 %copy-start.6 = (s32[64]{0:T(128)S(1)}, s32[64]{0:T(128)}, u32[]{:S(2)}) copy-start(s32[64]{0:T(128)} %param.14) | copy-start | bytes 772
  7.2 0.7 %copy-start.7 = (f32[64]{0:T(128)S(1)}, f32[64]{0:T(128)}, u32[]{:S(2)}) copy-start(f32[64]{0:T(128)} %param.15) | copy-start | bytes 772
  7.9 0.7 %copy-start.8 = (f32[32]{0:T(128)S(1)}, f32[32]{0:T(128)}, u32[]{:S(2)}) copy-start(f32[32]{0:T(128)} %param.17) | copy-start | bytes 388

commit v4 on v3

--- a/solution.py
+++ b/solution.py
@@ -72,15 +72,15 @@
     vel_hbm, start_ref, *refs,
 ):
     staged = refs[: 7 + tab_count]
-    upd, prs = refs[7 + tab_count : 9 + tab_count]
+    upd_hbm, prs_hbm = refs[7 + tab_count : 9 + tab_count]
     vel = refs[9 + tab_count]
     local_refs = refs[10 + tab_count : 17 + 2 * tab_count]
     tlevel, trow, tcol, thrust, green, shift, ramp_tab = local_refs[:7]
     tab_y, tab_x = local_refs[7], local_refs[-1]
     (
-        w_side, uv_side, h_src, h_side, fr_src, fr_buf, p_above,
+        upd, prs, zeros, w_side, uv_side, h_src, h_side, fr_src, fr_buf,
         spec, modes, back, planes, m_hi, m_lo, mt_hi, mt_lo, inv,
-        in_sem, halo_send, halo_recv, fr_send, fr_recv, pa_send, pa_recv,
+        in_sem, out_sem, halo_send, halo_recv, fr_send, fr_recv, pa_send, pa_recv,
         x_send, x_recv, y_send, y_recv,
     ) = refs[17 + 2 * tab_count :]
     levels, ny, nx = vel.shape[1:]
@@ -164,8 +164,6 @@
             w_side[side] = jnp.zeros((ny, nx), F32)
             h_side[side] = jnp.zeros((ny, nx), F32)
             uv_side[side] = jnp.zeros((2, ny, nx), F32)
-            if side == 1:
-                p_above[...] = jnp.zeros((ny, nx), F32)
 
     for load in loads:
         load.wait()
@@ -316,11 +314,13 @@
     for side in (inner, outer):
         edge = side * top
         receive(1, side)
+        if side is outer:
+            send(2, 0)
+            send(2, 1)
         prs[edge] = prs[edge] + h_side[side]
         transform(edge)
     for k in range(1, top):
         transform(k)
-    send(2, 1)
 
     scaled = None
     for k in range(top, -1, -1):
@@ -333,37 +333,48 @@
         own = pl.ds(k * ny, ny)
         put(back.at[k], left_mul(mt_hi[own], mt_lo[own], scaled), n)
         exchange(back.at[k], planes.at[k], y_send.at[k], y_recv.at[k])
-    send(2, 0)
-
-    receive(2, 0)
-    for c in range(2):
-        upd[c, 0] = upd[c, 0] + (half * keep) * (vel[2, 0] * uv_side[0, c])
-
-    p_down = remote(prs.at[0], p_above, pa_send, pa_recv, {"gz": down})
-
+    for side in range(2):
+        edge = side * top
+        signed = half * (2 * side - 1)
+        receive(2, side)
+        for c in range(2):
+            upd[c, edge] = upd[c, edge] - (signed * keep) * (vel[2, edge] * uv_side[side, c])
+    out_upd = pltpu.make_async_copy(upd, upd_hbm, out_sem.at[0])
+    out_upd.start()
+
+    p_down = remote(prs.at[0], prs_hbm.at[levels], pa_send, pa_recv, {"gz": down})
+    no_above = pltpu.make_async_copy(zeros, prs_hbm.at[levels], out_sem.at[1])
+
+    @pl.when(jnp.logical_not(there(1)))
+    def _():
+        zeros[...] = jnp.zeros((ny, nx), F32)
+        no_above.start()
+
+    out_prs = []
     for k in range(levels):
         arrived(planes.at[k], y_recv.at[k])
-        pressure = right_mul(left_mul(*rt_y, get(planes.at[k])), *r_x)
-        prs[k] = pressure
+        prs[k] = right_mul(left_mul(*rt_y, get(planes.at[k])), *r_x)
         if k == 0:
+
             @pl.when(there(0))
             def _():
                 p_down.start()
 
-        else:
-            upd[2, k - 1] = upd[2, k - 1] - (pressure - prs[k - 1])
-        if k == top:
-            receive(2, 1)
-            for c in range(2):
-                upd[c, top] = upd[c, top] - (half * keep) * (vel[2, top] * uv_side[1, c])
-        upd[0, k] = upd[0, k] - dx(pressure)
-        upd[1, k] = upd[1, k] - dy(pressure)
+        copy = pltpu.make_async_copy(prs.at[k], prs_hbm.at[k], out_sem.at[2 + k])
+        copy.start()
+        out_prs.append(copy)
 
     @pl.when(there(1))
     def _():
         p_down.wait_recv()
 
-    upd[2, top] = upd[2, top] - (p_above[...] - prs[top])
+    @pl.when(jnp.logical_not(there(1)))
+    def _():
+        no_above.wait()
+
+    out_upd.wait()
+    for copy in out_prs:
+        copy.wait()
 
     for side in range(2):
 
@@ -384,6 +395,45 @@
     for k in range(levels):
         sent(spec.at[k], x_send.at[k])
         sent(back.at[k], y_send.at[k])
+
+
+def correct(base_hbm, planes_hbm, dy_hbm, dx_hbm, upd_hbm, prs_hbm, upd, prs, d_y, d_x, sem, out_sem):
+    levels = prs_hbm.shape[0]
+    loads = [
+        pltpu.make_async_copy(src, dst, sem.at[i])
+        for i, (src, dst) in enumerate(
+            [(planes_hbm.at[k], prs.at[k]) for k in range(levels)]
+            + [
+                (dx_hbm, d_x),
+                (dy_hbm, d_y),
+                (base_hbm.at[pl.ds(0, 2)], upd.at[pl.ds(0, 2)]),
+                (planes_hbm.at[levels], prs.at[levels]),
+                (base_hbm.at[2], upd.at[2]),
+            ]
+        )
+    ]
+    for load in loads:
+        load.start()
+    whole = pltpu.make_async_copy(planes_hbm.at[pl.ds(0, levels)], prs_hbm, out_sem.at[levels])
+    whole.start()
+    for load in loads[: levels + 3]:
+        load.wait()
+    outs = []
+    uv = pl.ds(0, 2)
+    for k in range(levels):
+        pressure = prs[k]
+        upd[0, k] = upd[0, k] + right_mul(pressure, d_x[0], d_x[1])
+        upd[1, k] = upd[1, k] - left_mul(d_y[0], d_y[1], pressure)
+        outs.append(pltpu.make_async_copy(upd.at[uv, k], upd_hbm.at[uv, k], out_sem.at[k]))
+        outs[-1].start()
+    for load in loads[levels + 3 :]:
+        load.wait()
+    for k in range(levels):
+        upd[2, k] = upd[2, k] - (prs[k + 1] - prs[k])
+    last = pltpu.make_async_copy(upd.at[2], upd_hbm.at[2], sem.at[levels + 5])
+    last.start()
+    for copy in (whole, *outs, last):
+        copy.wait()
 
 
 def put(ref, value, n):
@@ -414,7 +464,6 @@
     offset = (np.arange(FRINGE) + 0.5)[:, None]
     ramp_tab = (np.sin(np.pi * offset / FRINGE) ** 2).astype(np.float32)
     hbm = pl.BlockSpec(memory_space=pltpu.HBM)
-    vmem = pl.BlockSpec(memory_space=pltpu.VMEM)
     smem = pl.BlockSpec(memory_space=pltpu.SMEM)
     plane = (n, rows, nx)
     dma = pltpu.SemaphoreType.DMA
@@ -424,23 +473,25 @@
         green_basis, eigen_shift[None], ramp_tab, *tabs,
     ]
     fields = velocity[0]
-    updated, pressure = pl.pallas_call(
+    base, planes = pl.pallas_call(
         functools.partial(kernel, n, groups, len(tabs)),
         out_shape=(
             jax.ShapeDtypeStruct((3, levels, ny, nx), F32),
-            jax.ShapeDtypeStruct((levels, ny, nx), F32),
+            jax.ShapeDtypeStruct((levels + 1, ny, nx), F32),
         ),
         in_specs=[hbm, smem] + [hbm] * len(staged),
-        out_specs=(vmem, vmem),
+        out_specs=(hbm, hbm),
         scratch_shapes=[pltpu.VMEM(x.shape, x.dtype) for x in (fields, *staged)]
         + [
+            pltpu.VMEM((3, levels, ny, nx), F32),
+            pltpu.VMEM((levels, ny, nx), F32),
+            pltpu.VMEM((ny, nx), F32),
             pltpu.VMEM((2, ny, nx), F32),
             pltpu.VMEM((2, 2, ny, nx), F32),
             pltpu.VMEM((2, ny, nx), F32),
             pltpu.VMEM((2, ny, nx), F32),
             pltpu.VMEM((2 * levels, FRINGE, ny), F32),
             pltpu.VMEM((2 * levels, FRINGE, ny), F32),
-            pltpu.VMEM((ny, nx), F32),
             pltpu.VMEM((levels, *plane), F32),
             pltpu.VMEM((levels, *plane), F32),
             pltpu.VMEM((levels, *plane), F32),
@@ -451,6 +502,7 @@
             pltpu.VMEM((nb, nb), BF16),
             pltpu.VMEM((nb, nx), F32),
             dma((1 + len(staged),)),
+            dma((2 + levels,)),
             dma((3, 2)),
             dma((3, 2)),
             dma((max(groups - 1, 1),)),
@@ -463,10 +515,30 @@
             dma((levels,)),
         ],
         compiler_params=pltpu.CompilerParams(
-            collective_id=0, has_side_effects=True, vmem_limit_bytes=40 * 1024 * 1024
+            collective_id=0, has_side_effects=True, vmem_limit_bytes=58 * 1024 * 1024
         ),
         name="fractional_step",
     )(fields, fringe_start, *staged)
+    derivs = [tab[4:] for tab in tabs]
+    updated, pressure = pl.pallas_call(
+        correct,
+        out_shape=(
+            jax.ShapeDtypeStruct((3, levels, ny, nx), F32),
+            jax.ShapeDtypeStruct((levels, ny, nx), F32),
+        ),
+        in_specs=[hbm] * 4,
+        out_specs=(hbm, hbm),
+        scratch_shapes=[
+            pltpu.VMEM((3, levels, ny, nx), F32),
+            pltpu.VMEM((levels + 1, ny, nx), F32),
+            pltpu.VMEM((2, ny, ny), BF16),
+            pltpu.VMEM((2, nx, nx), BF16),
+            dma((levels + 6,)),
+            dma((levels + 1,)),
+        ],
+        compiler_params=pltpu.CompilerParams(vmem_limit_bytes=58 * 1024 * 1024),
+        name="correction",
+    )(base, planes, derivs[0], derivs[-1])
     return updated[None], pressure[None]
 
 

time: 60.2 us -> 72.8 us (1.21)
  the two profiles are of different devices: /device:TPU:15 before, /device:TPU:23 now
where the time goes in v4:
time: 72.8 us; the launch traced here: 72.7 us
  Pallas kernels  71.4 us (98%)
  between operations  1.29 us (2%)
    pallas_call x1, Pallas kernels, local(): pl.pallas_call(functools.partial(kernel, n, groups, len(tabs)), out_shape...  54.3 us
    pallas_call x1, Pallas kernels, local(): pl.pallas_call(correct, out_shape=(jax.ShapeDtypeStruct((3, levels, ny, n...  17.1 us

profile of v4, /device:TPU:23, one launch (start us, length us, event | category | flops | bytes accessed | tf_op | source)
XLA Modules:
  0.0 72.7 jit_solution(491810930538107987)
XLA Ops:
  1.3 54.3 %fractional_step.1 = (f32[3,2,256,256]{3,2,1,0:T(8,128)}, f32[3,256,256]{2,1,0:T(8,128)}) custom-call(f32[3,2,256,256]{3,2,1,0:T(8,128)} %bitcast.8, s32[1]{0:T(128)S(6)} %copy.13.start_ref, s32[1,64]{1,0:T(1,128)} %bitcast.9, s32[1,64]{1,0:T(1,128)} %bitcast.10, s32[1,64]{1,0:T(1,128)} %bitcast.11, f32[1,64]{1,0:T(1,128)} %bitcast.12, f32[32,32]{1,0:T(8,128)} %refs_4_.1, ...), custom_call_target="tpu_custom_call" | custom-call | tf_op jit(solution)/shard_map/fractional_step/pallas_call | solution.py:476
  55.6 17.1 %correction.1 = (f32[3,2,256,256]{3,2,1,0:T(8,128)}, f32[2,256,256]{2,1,0:T(8,128)}) custom-call(f32[3,2,256,256]{3,2,1,0:T(8,128)} %get-tuple-element.6.base_hbm, f32[3,256,256]{2,1,0:T(8,128)} %get-tuple-element.7.planes_hbm, bf16[2,256,256]{2,1,0:T(8,128)(2,1)} %constant.8.clone.dy_hbm.dx_hbm, bf16[2,256,256]{2,1,0:T(8,128)(2,1)} %constant.8.clone.dy_hbm.dx_hbm), custom_call_target="tpu_custom_call" | custom-call | tf_op jit(solution)/shard_map/correction/pallas_call | solution.py:523

commit v5 on v4

--- a/solution.py
+++ b/solution.py
@@ -78,7 +78,7 @@
     tlevel, trow, tcol, thrust, green, shift, ramp_tab = local_refs[:7]
     tab_y, tab_x = local_refs[7], local_refs[-1]
     (
-        upd, prs, zeros, w_side, uv_side, h_src, h_side, fr_src, fr_buf,
+        upd, prs, p_above, w_side, uv_side, h_src, h_side, fr_src, fr_buf,
         spec, modes, back, planes, m_hi, m_lo, mt_hi, mt_lo, inv,
         in_sem, out_sem, halo_send, halo_recv, fr_send, fr_recv, pa_send, pa_recv,
         x_send, x_recv, y_send, y_recv,
@@ -112,6 +112,7 @@
         pl.semaphore_signal(
             barrier, inc=1, device_id={"group": lax.rem(group + off, groups)}, device_id_type=MESH
         )
+    loads[0].wait()
     pl.semaphore_wait(barrier, n - 1 + groups - 1)
 
     def remote(src, dst, send, recv, where):
@@ -139,10 +140,10 @@
 
     def halo_copy(kind, side):
         if kind == 0:
-            return halo(vel_hbm.at[2, side * top], w_side, kind, side)
+            return halo(vel.at[2, side * top], w_side, kind, side)
         if kind == 1:
             return halo(h_src.at[side], h_side, kind, side)
-        return halo(vel_hbm.at[uv, side * top], uv_side, kind, side)
+        return halo(vel.at[uv, side * top], uv_side, kind, side)
 
     def send(kind, side):
         @pl.when(there(side))
@@ -165,7 +166,7 @@
             h_side[side] = jnp.zeros((ny, nx), F32)
             uv_side[side] = jnp.zeros((2, ny, nx), F32)
 
-    for load in loads:
+    for load in loads[1:]:
         load.wait()
 
     start = start_ref[0]
@@ -342,13 +343,11 @@
     out_upd = pltpu.make_async_copy(upd, upd_hbm, out_sem.at[0])
     out_upd.start()
 
-    p_down = remote(prs.at[0], prs_hbm.at[levels], pa_send, pa_recv, {"gz": down})
-    no_above = pltpu.make_async_copy(zeros, prs_hbm.at[levels], out_sem.at[1])
+    p_down = remote(prs.at[0], p_above, pa_send, pa_recv, {"gz": down})
 
     @pl.when(jnp.logical_not(there(1)))
     def _():
-        zeros[...] = jnp.zeros((ny, nx), F32)
-        no_above.start()
+        p_above[...] = jnp.zeros((ny, nx), F32)
 
     out_prs = []
     for k in range(levels):
@@ -368,13 +367,12 @@
     def _():
         p_down.wait_recv()
 
-    @pl.when(jnp.logical_not(there(1)))
-    def _():
-        no_above.wait()
-
+    out_above = pltpu.make_async_copy(p_above, prs_hbm.at[levels], out_sem.at[1])
+    out_above.start()
     out_upd.wait()
     for copy in out_prs:
         copy.wait()
+    out_above.wait()
 
     for side in range(2):
 
@@ -414,10 +412,10 @@
     ]
     for load in loads:
         load.start()
-    whole = pltpu.make_async_copy(planes_hbm.at[pl.ds(0, levels)], prs_hbm, out_sem.at[levels])
-    whole.start()
     for load in loads[: levels + 3]:
         load.wait()
+    whole = pltpu.make_async_copy(prs.at[pl.ds(0, levels)], prs_hbm, out_sem.at[levels])
+    whole.start()
     outs = []
     uv = pl.ds(0, 2)
     for k in range(levels):

time: 72.8 us -> 59 us (0.81)
  Pallas kernels: 71.4 us -> 57.6 us
    pallas_call x1, Pallas kernels: 17.1 us -> 3.2 us  [local(): pl.pallas_call(correct, out_shape=(jax.ShapeDtypeStruct((3, levels, ny, n...]
where the time goes in v5:
time: 59 us; the launch traced here: 58.9 us
  Pallas kernels  57.6 us (98%)
  between operations  1.29 us (2%)
    pallas_call x1, Pallas kernels, local(): pl.pallas_call(functools.partial(kernel, n, groups, len(tabs)), out_shape...  54.4 us
    pallas_call x1, Pallas kernels, local(): pl.pallas_call(correct, out_shape=(jax.ShapeDtypeStruct((3, levels, ny, n...  3.2 us

profile of v5, /device:TPU:23, one launch (start us, length us, event | category | flops | bytes accessed | tf_op | source)
XLA Modules:
  0.0 58.9 jit_solution(7749108345587440878)
XLA Ops:
  1.3 54.4 %fractional_step.1 = (f32[3,2,256,256]{3,2,1,0:T(8,128)}, f32[3,256,256]{2,1,0:T(8,128)}) custom-call(f32[3,2,256,256]{3,2,1,0:T(8,128)} %bitcast.8, s32[1]{0:T(128)S(6)} %copy.13.start_ref, s32[1,64]{1,0:T(1,128)} %bitcast.9, s32[1,64]{1,0:T(1,128)} %bitcast.10, s32[1,64]{1,0:T(1,128)} %bitcast.11, f32[1,64]{1,0:T(1,128)} %bitcast.12, f32[32,32]{1,0:T(8,128)} %refs_4_.1, ...), custom_call_target="tpu_custom_call" | custom-call | tf_op jit(solution)/shard_map/fractional_step/pallas_call | solution.py:474
  55.7 3.2 %correction.1 = (f32[3,2,256,256]{3,2,1,0:T(8,128)}, f32[2,256,256]{2,1,0:T(8,128)}) custom-call(f32[3,2,256,256]{3,2,1,0:T(8,128)} %get-tuple-element.6.base_hbm, f32[3,256,256]{2,1,0:T(8,128)} %get-tuple-element.7.planes_hbm, bf16[2,256,256]{2,1,0:T(8,128)(2,1)} %constant.8.clone.dy_hbm.dx_hbm, bf16[2,256,256]{2,1,0:T(8,128)(2,1)} %constant.8.clone.dy_hbm.dx_hbm), custom_call_target="tpu_custom_call" | custom-call | tf_op jit(solution)/shard_map/correction/pallas_call | solution.py:521

commit v6 on v5

--- a/solution.py
+++ b/solution.py
@@ -315,13 +315,11 @@
     for side in (inner, outer):
         edge = side * top
         receive(1, side)
-        if side is outer:
-            send(2, 0)
-            send(2, 1)
         prs[edge] = prs[edge] + h_side[side]
         transform(edge)
     for k in range(1, top):
         transform(k)
+    send(2, 1)
 
     scaled = None
     for k in range(top, -1, -1):
@@ -329,6 +327,7 @@
         cols = pl.ds(k * ny, ny)
         term = left_mul(m_hi[:, cols], m_lo[:, cols], get(modes.at[k]))
         scaled = term if scaled is None else scaled + term
+    send(2, 0)
     scaled = scaled * inv[...]
     for k in range(levels):
         own = pl.ds(k * ny, ny)

time: 59 us -> 56.4 us (0.956)
  the two profiles are of different devices: /device:TPU:23 before, /device:TPU:1 now
where the time goes in v6:
time: 56.4 us; the launch traced here: 56.2 us
  Pallas kernels  54.9 us (97%)
  between operations  1.29 us (2%)
    pallas_call x1, Pallas kernels, local(): pl.pallas_call(functools.partial(kernel, n, groups, len(tabs)), out_shape...  51.7 us
    pallas_call x1, Pallas kernels, local(): pl.pallas_call(correct, out_shape=(jax.ShapeDtypeStruct((3, levels, ny, n...  3.19 us

profile of v6, /device:TPU:1, one launch (start us, length us, event | category | flops | bytes accessed | tf_op | source)
XLA Modules:
  0.0 56.2 jit_solution(13824191435366179527)
XLA Ops:
  1.3 51.7 %fractional_step.1 = (f32[3,2,256,256]{3,2,1,0:T(8,128)}, f32[3,256,256]{2,1,0:T(8,128)}) custom-call(f32[3,2,256,256]{3,2,1,0:T(8,128)} %bitcast.8, s32[1]{0:T(128)S(6)} %copy.13.start_ref, s32[1,64]{1,0:T(1,128)} %bitcast.9, s32[1,64]{1,0:T(1,128)} %bitcast.10, s32[1,64]{1,0:T(1,128)} %bitcast.11, f32[1,64]{1,0:T(1,128)} %bitcast.12, f32[32,32]{1,0:T(8,128)} %refs_4_.1, ...), custom_call_target="tpu_custom_call" | custom-call | tf_op jit(solution)/shard_map/fractional_step/pallas_call | solution.py:473
  53.0 3.2 %correction.1 = (f32[3,2,256,256]{3,2,1,0:T(8,128)}, f32[2,256,256]{2,1,0:T(8,128)}) custom-call(f32[3,2,256,256]{3,2,1,0:T(8,128)} %get-tuple-element.6.base_hbm, f32[3,256,256]{2,1,0:T(8,128)} %get-tuple-element.7.planes_hbm, bf16[2,256,256]{2,1,0:T(8,128)(2,1)} %constant.8.clone.dy_hbm.dx_hbm, bf16[2,256,256]{2,1,0:T(8,128)(2,1)} %constant.8.clone.dy_hbm.dx_hbm), custom_call_target="tpu_custom_call" | custom-call | tf_op jit(solution)/shard_map/correction/pallas_call | solution.py:520

commit v7 on v6

--- a/solution.py
+++ b/solution.py
@@ -97,9 +97,7 @@
         pltpu.make_async_copy(src, dst, in_sem.at[i])
         for i, (src, dst) in enumerate(zip((vel_hbm, *staged), (vel, *local_refs)))
     ]
-    for load in loads:
-        load.start()
-
+    loads[0].start()
     barrier = pltpu.get_barrier_semaphore()
 
     @pl.loop(1, n)
@@ -112,6 +110,8 @@
         pl.semaphore_signal(
             barrier, inc=1, device_id={"group": lax.rem(group + off, groups)}, device_id_type=MESH
         )
+    for load in loads[1:]:
+        load.start()
     loads[0].wait()
     pl.semaphore_wait(barrier, n - 1 + groups - 1)
 
@@ -221,7 +221,8 @@
         upd[c, k] = field + TIME_STEP * tend
 
     for k in range(levels):
-        predict(2, k)
+        for c in (2, 0, 1):
+            predict(c, k)
 
     half = 0.5 * TIME_STEP
 
@@ -247,11 +248,9 @@
         speed = speed + jnp.where(tlevel[...] == me * levels + k, here, 0.0)
     drag = (-TIME_STEP * is_farm) * thrust[...] * jnp.abs(speed) * speed
     for k in range(levels):
-        predict(0, k)
         placed = jnp.where(pick_row & (tlevel[...] == me * levels + k), drag, 0.0)
         ph, pw = split(placed)
         upd[0, k] = upd[0, k] + dot_nt(ph, pick_col) + dot_nt(pw, pick_col)
-        predict(1, k)
 
     @pl.when(group > 0)
     def _():
@@ -269,6 +268,35 @@
         if k > 0:
             divergence = divergence - upd[2, k - 1]
         prs[k] = divergence
+
+    def exchange(src, dst, send, recv):
+        pltpu.make_async_copy(src.at[me], dst.at[me], recv).start()
+
+        @pl.loop(0, n - 1)
+        def _(i):
+            odd = lax.rem(i, 2)
+            peer = lax.rem(me + n // 2 + (1 - 2 * odd) * ((i + 1) // 2), n)
+            remote(src.at[peer], dst.at[me], send, recv, {"gz": peer}).start()
+
+    def arrived(dst, recv):
+        pltpu.make_async_copy(dst, dst, recv).wait()
+
+    def sent(src, send):
+        most = src.at[pl.ds(0, n - 1)]
+        pltpu.make_async_copy(most, most, send).wait()
+
+    def transform(k):
+        put(spec.at[k], right_mul(left_mul(*r_y, prs[k]), *rt_x), n)
+        exchange(spec.at[k], modes.at[k], x_send.at[k], x_recv.at[k])
+
+    for side in (inner, outer):
+        edge = side * top
+        receive(1, side)
+        prs[edge] = prs[edge] + h_side[side]
+        transform(edge)
+    for k in range(1, top):
+        transform(k)
+    send(2, 1)
 
     rbits = rows.bit_length() - 1
     ybits = ny.bit_length() - 1
@@ -292,34 +320,6 @@
     ky = me * rows + (iota((nb, 1), 0) & (rows - 1))
     kx = iota((1, nx), 1)
     inv[...] = 1.0 / (shifts + (wave_square(ky, ny) + wave_square(kx, nx)))
-
-    def exchange(src, dst, send, recv):
-        pltpu.make_async_copy(src.at[me], dst.at[me], recv).start()
-
-        @pl.loop(1, n)
-        def _(off):
-            peer = lax.rem(me + off, n)
-            remote(src.at[peer], dst.at[me], send, recv, {"gz": peer}).start()
-
-    def arrived(dst, recv):
-        pltpu.make_async_copy(dst, dst, recv).wait()
-
-    def sent(src, send):
-        most = src.at[pl.ds(0, n - 1)]
-        pltpu.make_async_copy(most, most, send).wait()
-
-    def transform(k):
-        put(spec.at[k], right_mul(left_mul(*r_y, prs[k]), *rt_x), n)
-        exchange(spec.at[k], modes.at[k], x_send.at[k], x_recv.at[k])
-
-    for side in (inner, outer):
-        edge = side * top
-        receive(1, side)
-        prs[edge] = prs[edge] + h_side[side]
-        transform(edge)
-    for k in range(1, top):
-        transform(k)
-    send(2, 1)
 
     scaled = None
     for k in range(top, -1, -1):

time: 56.4 us -> 59.4 us (1.053)
  Pallas kernels: 54.9 us -> 57.9 us
    pallas_call x1, Pallas kernels: 51.7 us -> 54.7 us  [local(): pl.pallas_call(functools.partial(kernel, n, groups, len(tabs)), out_shape...]
where the time goes in v7:
time: 59.4 us; the launch traced here: 59.2 us
  Pallas kernels  57.9 us (97%)
  between operations  1.29 us (2%)
    pallas_call x1, Pallas kernels, local(): pl.pallas_call(functools.partial(kernel, n, groups, len(tabs)), out_shape...  54.7 us
    pallas_call x1, Pallas kernels, local(): pl.pallas_call(correct, out_shape=(jax.ShapeDtypeStruct((3, levels, ny, n...  3.19 us

profile of v7, /device:TPU:1, one launch (start us, length us, event | category | flops | bytes accessed | tf_op | source)
XLA Modules:
  0.0 59.2 jit_solution(10982491906396394219)
XLA Ops:
  1.3 54.7 %fractional_step.1 = (f32[3,2,256,256]{3,2,1,0:T(8,128)}, f32[3,256,256]{2,1,0:T(8,128)}) custom-call(f32[3,2,256,256]{3,2,1,0:T(8,128)} %bitcast.8, s32[1]{0:T(128)S(6)} %copy.13.start_ref, s32[1,64]{1,0:T(1,128)} %bitcast.9, s32[1,64]{1,0:T(1,128)} %bitcast.10, s32[1,64]{1,0:T(1,128)} %bitcast.11, f32[1,64]{1,0:T(1,128)} %bitcast.12, f32[32,32]{1,0:T(8,128)} %refs_4_.1, ...), custom_call_target="tpu_custom_call" | custom-call | tf_op jit(solution)/shard_map/fractional_step/pallas_call | solution.py:473
  56.0 3.2 %correction.1 = (f32[3,2,256,256]{3,2,1,0:T(8,128)}, f32[2,256,256]{2,1,0:T(8,128)}) custom-call(f32[3,2,256,256]{3,2,1,0:T(8,128)} %get-tuple-element.6.base_hbm, f32[3,256,256]{2,1,0:T(8,128)} %get-tuple-element.7.planes_hbm, bf16[2,256,256]{2,1,0:T(8,128)(2,1)} %constant.8.clone.dy_hbm.dx_hbm, bf16[2,256,256]{2,1,0:T(8,128)(2,1)} %constant.8.clone.dy_hbm.dx_hbm), custom_call_target="tpu_custom_call" | custom-call | tf_op jit(solution)/shard_map/correction/pallas_call | solution.py:520

commit v8 on v7

--- a/solution.py
+++ b/solution.py
@@ -269,13 +269,18 @@
             divergence = divergence - upd[2, k - 1]
         prs[k] = divergence
 
+    flips = [2**bit * (1 - 2 * lax.rem(me // 2**bit, 2)) for bit in range(n.bit_length() - 1)]
+
     def exchange(src, dst, send, recv):
         pltpu.make_async_copy(src.at[me], dst.at[me], recv).start()
 
         @pl.loop(0, n - 1)
         def _(i):
             odd = lax.rem(i, 2)
-            peer = lax.rem(me + n // 2 + (1 - 2 * odd) * ((i + 1) // 2), n)
+            mask = (1 - odd) * (n // 2 + i // 2) + odd * ((i + 1) // 2)
+            peer = me
+            for bit, flip in enumerate(flips):
+                peer = peer + lax.rem(mask // 2**bit, 2) * flip
             remote(src.at[peer], dst.at[me], send, recv, {"gz": peer}).start()
 
     def arrived(dst, recv):

time: 59.4 us -> 60 us (1.010)
  Pallas kernels: 57.9 us -> 58.5 us
where the time goes in v8:
time: 60 us; the launch traced here: 59.8 us
  Pallas kernels  58.5 us (98%)
  between operations  1.29 us (2%)
    pallas_call x1, Pallas kernels, local(): pl.pallas_call(functools.partial(kernel, n, groups, len(tabs)), out_shape...  55.3 us
    pallas_call x1, Pallas kernels, local(): pl.pallas_call(correct, out_shape=(jax.ShapeDtypeStruct((3, levels, ny, n...  3.19 us

profile of v8, /device:TPU:1, one launch (start us, length us, event | category | flops | bytes accessed | tf_op | source)
XLA Modules:
  0.0 59.8 jit_solution(7780965097177273896)
XLA Ops:
  1.3 55.3 %fractional_step.1 = (f32[3,2,256,256]{3,2,1,0:T(8,128)}, f32[3,256,256]{2,1,0:T(8,128)}) custom-call(f32[3,2,256,256]{3,2,1,0:T(8,128)} %bitcast.8, s32[1]{0:T(128)S(6)} %copy.13.start_ref, s32[1,64]{1,0:T(1,128)} %bitcast.9, s32[1,64]{1,0:T(1,128)} %bitcast.10, s32[1,64]{1,0:T(1,128)} %bitcast.11, f32[1,64]{1,0:T(1,128)} %bitcast.12, f32[32,32]{1,0:T(8,128)} %refs_4_.1, ...), custom_call_target="tpu_custom_call" | custom-call | tf_op jit(solution)/shard_map/fractional_step/pallas_call | solution.py:478
  56.6 3.2 %correction.1 = (f32[3,2,256,256]{3,2,1,0:T(8,128)}, f32[2,256,256]{2,1,0:T(8,128)}) custom-call(f32[3,2,256,256]{3,2,1,0:T(8,128)} %get-tuple-element.6.base_hbm, f32[3,256,256]{2,1,0:T(8,128)} %get-tuple-element.7.planes_hbm, bf16[2,256,256]{2,1,0:T(8,128)(2,1)} %constant.8.clone.dy_hbm.dx_hbm, bf16[2,256,256]{2,1,0:T(8,128)(2,1)} %constant.8.clone.dy_hbm.dx_hbm), custom_call_target="tpu_custom_call" | custom-call | tf_op jit(solution)/shard_map/correction/pallas_call | solution.py:525

commit v9 on v7

--- a/solution.py
+++ b/solution.py
@@ -272,10 +272,9 @@
     def exchange(src, dst, send, recv):
         pltpu.make_async_copy(src.at[me], dst.at[me], recv).start()
 
-        @pl.loop(0, n - 1)
-        def _(i):
-            odd = lax.rem(i, 2)
-            peer = lax.rem(me + n // 2 + (1 - 2 * odd) * ((i + 1) // 2), n)
+        @pl.loop(1, n)
+        def _(off):
+            peer = lax.rem(me + off, n)
             remote(src.at[peer], dst.at[me], send, recv, {"gz": peer}).start()
 
     def arrived(dst, recv):

time: 59.4 us -> 56.2 us (0.946)
  Pallas kernels: 57.9 us -> 54.6 us
    pallas_call x1, Pallas kernels: 54.7 us -> 51.4 us  [local(): pl.pallas_call(functools.partial(kernel, n, groups, len(tabs)), out_shape...]
where the time goes in v9:
time: 56.2 us; the launch traced here: 55.9 us
  Pallas kernels  54.6 us (97%)
  between operations  1.29 us (2%)
    pallas_call x1, Pallas kernels, local(): pl.pallas_call(functools.partial(kernel, n, groups, len(tabs)), out_shape...  51.4 us
    pallas_call x1, Pallas kernels, local(): pl.pallas_call(correct, out_shape=(jax.ShapeDtypeStruct((3, levels, ny, n...  3.2 us

profile of v9, /device:TPU:1, one launch (start us, length us, event | category | flops | bytes accessed | tf_op | source)
XLA Modules:
  0.0 55.9 jit_solution(1259145557114480983)
XLA Ops:
  1.3 51.4 %fractional_step.1 = (f32[3,2,256,256]{3,2,1,0:T(8,128)}, f32[3,256,256]{2,1,0:T(8,128)}) custom-call(f32[3,2,256,256]{3,2,1,0:T(8,128)} %bitcast.8, s32[1]{0:T(128)S(6)} %copy.13.start_ref, s32[1,64]{1,0:T(1,128)} %bitcast.9, s32[1,64]{1,0:T(1,128)} %bitcast.10, s32[1,64]{1,0:T(1,128)} %bitcast.11, f32[1,64]{1,0:T(1,128)} %bitcast.12, f32[32,32]{1,0:T(8,128)} %refs_4_.1, ...), custom_call_target="tpu_custom_call" | custom-call | tf_op jit(solution)/shard_map/fractional_step/pallas_call | solution.py:472
  52.7 3.2 %correction.1 = (f32[3,2,256,256]{3,2,1,0:T(8,128)}, f32[2,256,256]{2,1,0:T(8,128)}) custom-call(f32[3,2,256,256]{3,2,1,0:T(8,128)} %get-tuple-element.6.base_hbm, f32[3,256,256]{2,1,0:T(8,128)} %get-tuple-element.7.planes_hbm, bf16[2,256,256]{2,1,0:T(8,128)(2,1)} %constant.8.clone.dy_hbm.dx_hbm, bf16[2,256,256]{2,1,0:T(8,128)(2,1)} %constant.8.clone.dy_hbm.dx_hbm), custom_call_target="tpu_custom_call" | custom-call | tf_op jit(solution)/shard_map/correction/pallas_call | solution.py:519
